TPU v7x, 128 devices: a whole 4x4x4 slice. The times are simulated.
128 devices in a mesh: row: 8 (over y, core), col: 16 (over x, z).
Axes of the slice: x: 4, y: 4, z: 4, core: 2. Of those that a mesh axis runs over, the one named last changes fastest.
Arguments:
- forcing: bfloat16 [8, 1048576], P(None, ('row', 'col')), may hold values from 0 to 1
- owner: int32 [1048576], P(('row', 'col')), may hold values from 0 to 127, as said below
- column: int32 [1048576], P(('row', 'col')), may hold values from 0 to 127
- area: float32 [1048576], P(('row', 'col')), may hold values from 0.25 to 2
- sunlit: int32 [1048576], P(('row', 'col')), may hold values 0 or 1
- plant_type: int32 [1048576], P(('row', 'col')), may hold values from 0 to 15
- leaf_area: float32 [1048576], P(('row', 'col')), may hold values from 0.5 to 6
- soil_water: float32 [15, 1048576], P(None, ('row', 'col')), may hold values from 0.1 to 0.4
- pft_table: float32 [4, 16], replicated, may hold values from 0 to 1
Outputs:
- atm_flux: float32 [4, 262144], P(None, ('row', 'col'))
- soil_after: float32 [15, 1048576], P(None, ('row', 'col'))
Inputs may be any that keep to these rules, and one draw needn't show every extreme that they name: Every device owns exactly 8192 rows; the rows of one device name one owner at most 80 times, and exactly 80 times for some device and owner in every draw.
All inputs are finite; a program needn't handle non-finite values. No bound on the sum of `sunlit` on one device may be relied on, other than what follows from the above.
Results may differ from a plain program's by a relative error of at most 0.0018.
Values may be sent and summed in bfloat16 or wider, within the bound.
A program may use at most 64 MiB of HBM per device.

v0:
```python
import math

import jax
import jax.numpy as jnp
from jax import lax
from jax.sharding import PartitionSpec as P

NOUT = 4
NPFT = 16
LEVELS = 15
ITERS = 4
SOILP = 4
BROWS = 512
BCOLS = 128


def land_physics(fields, sunlit_f, params, leaf_area, theta):
    omega = 0.1 + 0.3 * params[0]
    vcmax = 0.5 + 1.5 * params[1]
    slope = 3.0 + 6.0 * params[2]
    kroot = 0.05 + 0.5 * params[3]
    swdir = 2.0 * fields[0]
    swdif = fields[1]
    tair = fields[2] - 0.5
    vapour = 0.2 + fields[3]
    carbon = 0.8 + 0.4 * fields[4]
    coszen = 0.1 + 0.9 * fields[5]
    wind_speed = 0.5 + 2.0 * fields[6]
    precip = fields[7]
    single = jnp.sqrt(1.0 - omega)
    extinct = 0.5 / coszen
    reflect_h = (1.0 - single) / (1.0 + single)
    reflect_b = 2.0 * extinct * reflect_h / (1.0 + extinct)
    light = sunlit_f * (
        (1.0 - reflect_b) * swdir * (1.0 - jnp.exp(-extinct * single * leaf_area))
        + (1.0 - reflect_h) * swdif * (1.0 - jnp.exp(-0.8 * single * leaf_area))
    )
    electrons = 0.3 * light
    compensation = 0.08 * (1.0 + 0.3 * tair)
    capacity_t = vcmax * jnp.exp(0.5 * tair)
    internal = 0.7 * carbon
    assim = jnp.zeros_like(internal)
    conduct = jnp.zeros_like(internal)
    for repeat in range(ITERS):
        limit = internal - compensation
        carboxyl = capacity_t * limit / (internal + 0.6)
        ribulose = electrons * limit / (4.0 * internal + 8.0 * compensation)
        assim = carboxyl * ribulose / (carboxyl + ribulose)
        conduct = 0.05 + slope * assim / carbon
        internal = carbon - 1.6 * assim / conduct
    transpire = conduct * vapour
    sensible = 0.5 * wind_speed * (0.2 * light - 0.5 * transpire)
    depths = jnp.arange(LEVELS, dtype=jnp.float32)
    roots = jnp.exp(-kroot[None, :] * depths[:, None])
    roots = roots / jnp.sum(roots, axis=0, keepdims=True)
    theta = jnp.concatenate([theta[:1] + 0.1 * precip[None, :], theta[1:]], axis=0)
    for repeat in range(SOILP):
        above = jnp.concatenate([theta[:1], theta[:-1]], axis=0)
        below = jnp.concatenate([theta[1:], theta[-1:]], axis=0)
        theta = theta + 0.25 * (above + below - 2.0 * theta) - 0.05 * transpire[None, :] * roots
    drainage = 0.5 * theta[LEVELS - 1]
    tile_flux = jnp.stack([assim, transpire, sensible, drainage], axis=0).astype(jnp.bfloat16)
    return (tile_flux, theta)


def block_sums(weighted, column):
    rows_here = weighted.shape[1]
    blocks = rows_here // BROWS
    group = math.gcd(16, blocks)
    turns = blocks // group
    values = jnp.moveaxis(weighted.reshape(NOUT, turns, group, BROWS), 1, 0)
    targets = column.reshape(turns, group, BROWS)
    labels = jnp.arange(BCOLS, dtype=jnp.int32)

    def one_group(pair):
        block_vals, block_cols = pair
        onehot = (block_cols[:, :, None] == labels[None, None, :]).astype(jnp.float32)
        return jnp.einsum("jgr,grc->jgc", block_vals, onehot, precision=lax.Precision.HIGHEST)

    summed = lax.map(one_group, (values, targets))
    return jnp.moveaxis(summed, 0, 1).reshape(NOUT, blocks * BCOLS)


def body(forcing, owner, column, area, sunlit, plant_type, leaf_area, soil_water, pft_table):
    peer_count = lax.axis_size(("row", "col"))
    fields_n = forcing.shape[0]
    rows_here = forcing.shape[1]
    mean_rows = rows_here // peer_count
    capacity = mean_rows + mean_rows // 4
    peer_ids = jnp.arange(peer_count, dtype=jnp.int32)
    slot_ids = jnp.arange(capacity, dtype=jnp.int32)
    row_ids = jnp.arange(rows_here, dtype=jnp.int32)
    order = jnp.argsort(owner, stable=True)
    send_counts = jnp.sum((owner[None, :] == peer_ids[:, None]).astype(jnp.int32), axis=1)
    send_starts = jnp.cumsum(send_counts) - send_counts
    send_valid = slot_ids[None, :] < send_counts[:, None]
    send_pick = jnp.clip(send_starts[:, None] + slot_ids[None, :], 0, rows_here - 1)
    picked = forcing[:, order[send_pick].reshape(-1)].reshape(fields_n, peer_count, capacity)
    outgoing = jnp.where(send_valid[None], picked, jnp.zeros((), jnp.bfloat16))
    sorted_dest = owner[order]
    sorted_pos = sorted_dest * capacity + row_ids - send_starts[sorted_dest]
    row_place = jnp.zeros((rows_here,), jnp.int32).at[order].set(sorted_pos)
    count_note = send_counts.reshape(1, peer_count, 1)
    arrived, arrived_counts = (
        lax.all_to_all(outgoing, ("row", "col"), split_axis=1, concat_axis=1, tiled=True),
        lax.all_to_all(count_note, ("row", "col"), split_axis=1, concat_axis=1, tiled=True),
    )
    arrived = arrived.reshape(fields_n, peer_count * capacity)
    arrived_counts = arrived_counts.reshape(peer_count)
    recv_ends = jnp.cumsum(arrived_counts)
    recv_starts = recv_ends - arrived_counts
    passed = row_ids[:, None] >= recv_ends[None, :]
    buffer_index = row_ids + jnp.sum(
        jnp.where(passed, capacity - arrived_counts[None, :], 0), axis=1
    )
    tile_fields = arrived[:, buffer_index].astype(jnp.float32)
    type_onehot = (plant_type[None, :] == jnp.arange(NPFT, dtype=jnp.int32)[:, None]).astype(
        jnp.float32
    )
    params = jnp.dot(pft_table, type_onehot, precision=lax.Precision.HIGHEST)
    tile_flux, soil_after = land_physics(
        tile_fields, sunlit.astype(jnp.float32), params, leaf_area, soil_water
    )
    back_valid = slot_ids[None, :] < arrived_counts[:, None]
    back_pick = jnp.clip(recv_starts[:, None] + slot_ids[None, :], 0, rows_here - 1)
    back_vals = tile_flux[:, back_pick.reshape(-1)].reshape(NOUT, peer_count, capacity)
    homeward = jnp.where(back_valid[None], back_vals, jnp.zeros((), jnp.bfloat16))
    returned = lax.all_to_all(homeward, ("row", "col"), split_axis=1, concat_axis=1, tiled=True)
    returned = returned.reshape(NOUT, peer_count * capacity)
    row_flux = returned[:, row_place].astype(jnp.float32)
    weighted = row_flux * area[None, :]
    atm_flux = block_sums(weighted, column)
    return (atm_flux, soil_after)


def solution(mesh):
    return jax.shard_map(
        body,
        mesh=mesh,
        in_specs=(
            P(None, ("row", "col")),
            P(("row", "col")),
            P(("row", "col")),
            P(("row", "col")),
            P(("row", "col")),
            P(("row", "col")),
            P(("row", "col")),
            P(None, ("row", "col")),
            P(),
        ),
        out_specs=(P(None, ("row", "col")), P(None, ("row", "col"))),
        check_vma=False,
    )
```

profile of v0, /device:TPU:1, one launch (start us, length us, event | category | flops | bytes accessed | tf_op | source)
XLA Modules:
  0.0 401.4 jit_solution(13204021524890971344)
XLA Ops:
  0.6 1.3 convert_reduce_fusion
  1.9 0.7 copy.45
  2.6 11.5 %all-to-all-start = ((s32[1,128,1]{2,0,1:T(1,128)}), s32[1,128,1]{2,0,1:T(1,128)S(1)}, u32[]{:S(2)}, u32[]{:S(2)}) async-start(s32[1,128,1]{2,0,1:T(1,128)} %copy.45), calls=%async_computation | async-start | bytes 131072 | tf_op jit(solution)/shard_map/all_to_all | solution.py:106
  14.9 7.5 %sort.17 = (s32[8192]{0:T(1024)}, s32[8192]{0:T(1024)S(1)}) sort(s32[8192]{0:T(1024)} %param.10, s32[8192]{0:T(1024)S(1)} %iota.46), dimensions={0}, to_apply=%region_1.2 | sort | flops 106496 | bytes 131072 | tf_op jit(solution)/shard_map/jit(argsort)/sort | solution.py:93
  22.4 56.8 %gather_fusion = s32[10240]{0:T(1024)S(1)} fusion(s32[8192]{0:T(1024)S(1)} %get-tuple-element.13, s32[10240]{0:T(1024)S(1)} %broadcast_clamp_fusion.1), kind=kCustom, calls=%fused_computation | custom fusion | bytes 122880 | tf_op jit(solution)/shard_map/gather | solution.py:98
  79.3 1.0 copy.47
  80.3 36.2 %gather_fusion.1 = bf16[10240,8]{1,0:T(8,128)(2,1)} fusion(bf16[8,8192]{0,1:T(8,128)(2,1)S(1)} %copy.47, s32[10240]{0:T(1024)S(1)} %broadcast_clamp_fusion.2), kind=kCustom, calls=%fused_computation.1 | custom fusion | bytes 368640 | tf_op jit(solution)/shard_map/gather | solution.py:98
  116.5 2.1 copy.48
  118.6 45.5 %gather_fusion.4 = s32[8192]{0:T(1024)S(1)} fusion(s32[8192]{0:T(1024)S(1)} %copy-done.1, s32[8192]{0:T(1024)S(1)} %get-tuple-element.52), kind=kCustom, calls=%fused_computation.4 | custom fusion | bytes 98304 | tf_op jit(solution)/shard_map/gather | solution.py:100
  164.3 48.9 %gather_fusion.5 = s32[8192]{0:T(1024)S(1)} fusion(s32[128]{0:T(128)S(1)} %sub.98, s32[8192]{0:T(1024)S(1)} %broadcast_clamp_fusion.3), kind=kCustom, calls=%fused_computation.5 | custom fusion | bytes 98304 | tf_op jit(solution)/shard_map/gather | solution.py:101
  213.1 0.8 broadcast_select_fusion
  214.3 31.0 %scatter_custom_fusion = s32[8192]{0:T(1024)} fusion(s32[8192]{0:T(1024)S(1)} %get-tuple-element.53, s32[8192]{0:T(1024)S(1)} %add_subtract_fusion, s32[]{:T(128)} %constant.31.clone.1), kind=kCustom, calls=%fused_computation.108 | custom fusion | bytes 32772 | tf_op jit(solution)/shard_map/scatter | solution.py:102
  245.3 9.8 %all-to-all-start.1 = ((bf16[8,128,80]{2,0,1:T(8,128)(2,1)}), bf16[8,128,80]{2,0,1:T(8,128)(2,1)S(1)}, u32[]{:S(2)}, u32[]{:S(2)}) async-start(bf16[8,128,80]{2,0,1:T(8,128)(2,1)} %broadcast_select_fusion), calls=%async_computation.1 | async-start | bytes 524288 | tf_op jit(solution)/shard_map/all_to_all | solution.py:105
  255.4 2.4 reduce
  257.7 1.2 select_reduce_fusion
  260.5 0.7 iota_compare_fusion.9
  261.2 4.8 %all-to-all-done.1 = bf16[8,128,80]{2,0,1:T(8,128)(2,1)S(1)} async-done(((bf16[8,128,80]{2,0,1:T(8,128)(2,1)}), bf16[8,128,80]{2,0,1:T(8,128)(2,1)S(1)}, u32[]{:S(2)}, u32[]{:S(2)}) %all-to-all-start.1) | async-done | bytes 163872 | tf_op jit(solution)/shard_map/all_to_all | solution.py:105
  265.9 1.1 copy.49
  267.1 31.9 %gather_fusion.2 = bf16[8192,8]{1,0:T(8,128)(2,1)} fusion(bf16[8,10240]{0,1:T(8,128)(2,1)S(1)} %bitcast.45, s32[8192]{0:T(1024)} %broadcast_clamp_fusion.5), kind=kCustom, calls=%fused_computation.2 | custom fusion | bytes 294912 | tf_op jit(solution)/shard_map/gather | solution.py:116
  299.0 1.8 copy.51
  301.4 1.4 fusion.54
  306.0 1.1 copy.52
  307.0 36.2 %gather_fusion.3 = bf16[10240,4]{1,0:T(8,128)(2,1)} fusion(bf16[4,8192]{0,1:T(8,128)(2,1)S(1)} %copy.52, s32[10240]{0:T(1024)S(1)} %copy-done.4), kind=kCustom, calls=%fused_computation.3 | custom fusion | bytes 204800 | tf_op jit(solution)/shard_map/gather | solution.py:126
  343.2 2.4 copy.53
  345.6 0.8 broadcast_select_fusion.1
  346.4 5.0 %all-to-all-start.2 = ((bf16[4,128,80]{2,0,1:T(4,128)(2,1)}), bf16[4,128,80]{2,0,1:T(4,128)(2,1)S(1)}, u32[]{:S(2)}, u32[]{:S(2)}) async-start(bf16[4,128,80]{2,0,1:T(4,128)(2,1)} %broadcast_select_fusion.1), calls=%async_computation.2 | async-start | bytes 262144 | tf_op jit(solution)/shard_map/all_to_all | solution.py:128
  351.5 9.8 %all-to-all-done.2 = bf16[4,128,80]{2,0,1:T(4,128)(2,1)S(1)} async-done(((bf16[4,128,80]{2,0,1:T(4,128)(2,1)}), bf16[4,128,80]{2,0,1:T(4,128)(2,1)S(1)}, u32[]{:S(2)}, u32[]{:S(2)}) %all-to-all-start.2) | async-done | bytes 81952 | tf_op jit(solution)/shard_map/all_to_all | solution.py:128
  361.3 1.2 copy.54
  362.5 29.2 %gather_fusion.6 = bf16[8192,4]{1,0:T(8,128)(2,1)} fusion(bf16[4,10240]{0,1:T(8,128)(2,1)S(1)} %bitcast.46, s32[8192]{0:T(1024)S(1)} %fusion.25), kind=kCustom, calls=%fused_computation.6 | custom fusion | bytes 163840 | tf_op jit(solution)/shard_map/gather | solution.py:130
  391.7 3.8 convert_element_type.27
  395.5 2.8 copy.55
  398.4 3.0 fusion.1
  (79 shorter events, 6.6 us)
Async XLA Ops:
  0.6 213.3 %copy-start = (f32[4,16]{1,0:T(4,128)S(1)}, f32[4,16]{1,0:T(4,128)}, u32[]{:S(2)}) copy-start(f32[4,16]{1,0:T(4,128)} %param.17) | copy-start | bytes 772
  2.6 242.7 %all-to-all-start = ((s32[1,128,1]{2,0,1:T(1,128)}), s32[1,128,1]{2,0,1:T(1,128)S(1)}, u32[]{:S(2)}, u32[]{:S(2)}) async-start(s32[1,128,1]{2,0,1:T(1,128)} %copy.45), calls=%async_computation | async-start | bytes 131072 | tf_op jit(solution)/shard_map/all_to_all | solution.py:106
  22.4 56.9 %copy-start.5 = (bf16[8,8192]{1,0:T(8,128)(2,1)S(1)}, bf16[8,8192]{1,0:T(8,128)(2,1)}, u32[]{:S(2)}) copy-start(bf16[8,8192]{1,0:T(8,128)(2,1)} %param.9) | copy-start | bytes 393220
  80.3 38.3 %copy-start.1 = (s32[8192]{0:T(1024)S(1)}, s32[8192]{0:T(1024)}, u32[]{:S(2)}) copy-start(s32[8192]{0:T(1024)} %param.10) | copy-start | bytes 98308
  164.2 49.7 %copy-start.12 = (s32[8192]{0:T(1024)S(1)}, s32[8192]{0:T(1024)}, u32[]{:S(2)}) copy-start(s32[8192]{0:T(1024)} %param.14) | copy-start | bytes 98308
  164.3 50.0 %copy-start.2 = (f32[15,8192]{1,0:T(8,128)S(1)}, f32[15,8192]{1,0:T(8,128)}, u32[]{:S(2)}) copy-start(f32[15,8192]{1,0:T(8,128)} %param.16) | copy-start | bytes 1474564
  245.3 20.6 %all-to-all-start.1 = ((bf16[8,128,80]{2,0,1:T(8,128)(2,1)}), bf16[8,128,80]{2,0,1:T(8,128)(2,1)S(1)}, u32[]{:S(2)}, u32[]{:S(2)}) async-start(bf16[8,128,80]{2,0,1:T(8,128)(2,1)} %broadcast_select_fusion), calls=%async_computation.1 | async-start | bytes 524288 | tf_op jit(solution)/shard_map/all_to_all | solution.py:105
  267.1 35.8 %copy-start.8 = (f32[8192]{0:T(1024)S(1)}, f32[8192]{0:T(1024)}, u32[]{:S(2)}) copy-start(f32[8192]{0:T(1024)} %param.15) | copy-start | bytes 98308
  267.1 35.8 %copy-start.9 = (s32[8192]{0:T(1024)S(1)}, s32[8192]{0:T(1024)}, u32[]{:S(2)}) copy-start(s32[8192]{0:T(1024)} %param.13) | copy-start | bytes 98308
  304.6 2.5 copy-start.4
  305.0 0.8 copy-start.3
  305.9 39.7 %copy-start.7 = (pred[128,80]{1,0:T(8,128)(4,1)S(1)}, pred[128,80]{1,0:T(8,128)(4,1)}, u32[]{:S(2)}) copy-start(pred[128,80]{1,0:T(8,128)(4,1)} %iota_compare_fusion.9) | copy-start | bytes 30724
  305.9 45.5 %copy-start.6 = (s32[8192]{0:T(1024)S(1)}, s32[8192]{0:T(1024)}, u32[]{:S(2)}) copy-start(s32[8192]{0:T(1024)} %scatter_custom_fusion) | copy-start | bytes 98308
  305.9 45.5 %copy-start.10 = (s32[8192]{0:T(1024)S(1)}, s32[8192]{0:T(1024)}, u32[]{:S(2)}) copy-start(s32[8192]{0:T(1024)} %param.11) | copy-start | bytes 98308
  307.0 44.4 %copy-start.11 = (f32[8192]{0:T(1024)S(1)}, f32[8192]{0:T(1024)}, u32[]{:S(2)}) copy-start(f32[8192]{0:T(1024)} %param.12) | copy-start | bytes 98308
  346.4 14.9 %all-to-all-start.2 = ((bf16[4,128,80]{2,0,1:T(4,128)(2,1)}), bf16[4,128,80]{2,0,1:T(4,128)(2,1)S(1)}, u32[]{:S(2)}, u32[]{:S(2)}) async-start(bf16[4,128,80]{2,0,1:T(4,128)(2,1)} %broadcast_select_fusion.1), calls=%async_computation.2 | async-start | bytes 262144 | tf_op jit(solution)/shard_map/all_to_all | solution.py:128
where the time goes:
time: 403 us; the launch traced here: 401 us
  local copies, waits for them, and re-layouts  332 us (82%)
  starting transfers between devices  26.3 us (7%)
  other arithmetic  24.4 us (6%)
  waiting for transfers between devices  14.6 us (4%)
    gather x1, local copies, waits for them, and re-layouts, body(): order[send_pick].reshape(-1)  56.8 us
    gather x1, local copies, waits for them, and re-layouts, body(): sorted_pos = sorted_dest * capacity + row_ids - send_starts[sorted_dest]  48.9 us
    gather x1, local copies, waits for them, and re-layouts, body(): sorted_dest = owner[order]  45.5 us
    gather x1, local copies, waits for them, and re-layouts, body(): forcing[:, order[send_pick].reshape(-1)]  36.2 us
    gather x1, local copies, waits for them, and re-layouts, body(): tile_flux[:, back_pick.reshape(-1)].reshape(NOUT, peer_count, capacity)  36.2 us
    gather x2, local copies, waits for them, and re-layouts, body(): tile_fields = arrived[:, buffer_index].astype(jnp.float32)  33.8 us
    scatter x1, local copies, waits for them, and re-layouts, body(): row_place = jnp.zeros((rows_here,), jnp.int32).at[order].set(sorted_pos)  31 us
    gather x1, local copies, waits for them, and re-layouts, body(): row_flux = returned[:, row_place].astype(jnp.float32)  29.2 us
  transfers between devices with their start and end apart: 3, of which 2 were waited for; matrix products, arithmetic and copies ran while one was open for 59% of the time, Pallas kernels for 0%

commit v1 on v0

v1 whole, which is shorter than its diff:
```python
import functools

import jax
import jax.numpy as jnp
from jax import lax
from jax.experimental import pallas as pl
from jax.experimental.pallas import tpu as pltpu
from jax.sharding import PartitionSpec as P

NF = 8
NOUT = 4
NPFT = 16
LEVELS = 15
ITERS = 4
SOILP = 4
BROWS = 512
BCOLS = 128
PEERS = 128
ROWS = 8192
LINES = ROWS // 128
SLOTS = 80
STEP = 256
WIDE = 1024
MESH = pl.DeviceIdType.MESH
F32 = jnp.float32
BF16 = jnp.bfloat16
NT = (((1,), (1,)), ((), ()))


def iota(shape, dim):
    return lax.broadcasted_iota(jnp.int32, shape, dim)


def as_bf16(mask):
    return jnp.where(mask, 1.0, 0.0).astype(BF16)


def dot(a, b):
    return jnp.dot(a, b, preferred_element_type=F32)


def dot_nt(a, b):
    return lax.dot_general(a, b, NT, preferred_element_type=F32)


def spread(hot, row):
    width = row.shape[1]
    tile = jnp.broadcast_to(row, (16, width)).astype(BF16)
    parts = hot.reshape(SLOTS // 16, 16, width) * tile[None]
    return parts.reshape(SLOTS, width)


def pack_kernel(owner_ref, forcing_ref, msg_ref, rank_ref, at_ref, w_ref, acc_ref):
    ids = iota((PEERS, 128), 0)
    for j in range(LINES):
        at_ref[:, 128 * j : 128 * j + 128] = as_bf16(ids == owner_ref[j : j + 1, :])
    base = jnp.zeros((PEERS, 128), F32)
    for g in range(ROWS // WIDE):
        earlier = as_bf16((iota((WIDE, 128), 0) + g * WIDE) // STEP < iota((WIDE, 128), 1))
        base = base + dot(at_ref[:, g * WIDE : (g + 1) * WIDE], earlier)
    upper = as_bf16(iota((STEP, STEP), 0) < iota((STEP, STEP), 1))
    slot = iota((SLOTS, STEP), 0).astype(F32)
    w_ref[NF * SLOTS :, :] = jnp.ones((16, WIDE), BF16)
    for g in range(ROWS // WIDE):
        for k in range(WIDE // STEP):
            c = g * (WIDE // STEP) + k
            a = at_ref[:, c * STEP : (c + 1) * STEP]
            seen = dot(a, upper) + base[:, c : c + 1]
            rank = jnp.sum(a.astype(F32) * seen, axis=0, keepdims=True)
            rank_ref[2 * c : 2 * c + 1, :] = rank[:, :128]
            rank_ref[2 * c + 1 : 2 * c + 2, :] = rank[:, 128:]
            hot = as_bf16(slot == rank)
            x = forcing_ref[:, c * STEP : (c + 1) * STEP].astype(F32)
            for f in range(NF):
                w_ref[f * SLOTS : (f + 1) * SLOTS, k * STEP : (k + 1) * STEP] = spread(hot, x[f : f + 1, :])
        part = dot_nt(w_ref[...], at_ref[:, g * WIDE : (g + 1) * WIDE])
        if g == 0:
            acc_ref[...] = part
        else:
            acc_ref[...] += part
    counts = acc_ref[NF * SLOTS : NF * SLOTS + 1, :]
    held = iota((SLOTS, PEERS), 0).astype(F32) < counts
    acc_ref[:SLOTS, :] = jnp.where(held, acc_ref[:SLOTS, :], -1.0)
    for i in range(NF * SLOTS // 128):
        msg_ref[pl.ds(i, PEERS, stride=8), :] = acc_ref[128 * i : 128 * (i + 1), :].T


def exchange_kernel(lines, cols, in_ref, out_ref, send_sem, recv_sem):
    me = lax.axis_index("row") * cols + lax.axis_index("col")
    barrier = pltpu.get_barrier_semaphore()

    def place(p):
        to = lax.rem(me + p, PEERS)
        return to, (to // cols, lax.rem(to, cols))

    def greet(p, carry):
        pl.semaphore_signal(barrier, inc=1, device_id=place(p)[1], device_id_type=MESH)
        return carry

    lax.fori_loop(1, PEERS, greet, 0)
    pl.semaphore_wait(barrier, PEERS - 1)
    own = pltpu.make_async_copy(in_ref.at[me, :lines], out_ref.at[me, :lines], recv_sem)
    own.start()

    def send(p, carry):
        to, device = place(p)
        pltpu.make_async_remote_copy(
            src_ref=in_ref.at[to, :lines],
            dst_ref=out_ref.at[me, :lines],
            send_sem=send_sem,
            recv_sem=recv_sem,
            device_id=device,
            device_id_type=MESH,
        ).start()
        return carry

    lax.fori_loop(1, PEERS, send, 0)
    sent = in_ref.at[: PEERS - 1, :lines]
    pltpu.make_async_copy(sent, sent, send_sem).wait()
    got = out_ref.at[:, :lines]
    pltpu.make_async_copy(got, got, recv_sem).wait()


def exchange(message, lines, cols, ident):
    return pl.pallas_call(
        functools.partial(exchange_kernel, lines, cols),
        out_shape=jax.ShapeDtypeStruct((PEERS, 8, 128), F32),
        in_specs=[pl.BlockSpec(memory_space=pl.ANY)],
        out_specs=pl.BlockSpec(memory_space=pl.ANY),
        scratch_shapes=[pltpu.SemaphoreType.DMA, pltpu.SemaphoreType.DMA],
        compiler_params=pltpu.CompilerParams(collective_id=ident, has_side_effects=True),
    )(message.reshape(PEERS, 8, 128)).reshape(PEERS * 8, 128)


def unfold(recv_ref, out_ref, lines):
    for i in range(lines):
        out_ref[128 * i : 128 * (i + 1), :] = recv_ref[pl.ds(i, PEERS, stride=8), :].T


def land_kernel(
    recv_ref, sunlit_ref, type_ref, leaf_ref, soil_ref, table_ref,
    msg_ref, after_ref,
    got_ref, p_ref, q_ref, field_ref, flux_ref, w_ref, acc_ref,
):
    unfold(recv_ref, acc_ref, NF * SLOTS // 128)
    counts = jnp.sum(jnp.where(acc_ref[:SLOTS, :] >= 0.0, 1.0, 0.0), axis=0, keepdims=True)
    below = iota((PEERS, PEERS), 1) < iota((PEERS, PEERS), 0)
    upto = iota((PEERS, PEERS), 1) <= iota((PEERS, PEERS), 0)
    after = as_bf16(iota((PEERS, PEERS), 0) < iota((PEERS, PEERS), 1))
    ones = jnp.ones((PEERS, STEP), BF16)
    begin = dot(jnp.where(below, counts, 0.0).astype(BF16), ones)
    end = dot(jnp.where(upto, counts, 0.0).astype(BF16), ones)
    begin_row = dot(jnp.broadcast_to(counts, (16, PEERS)).astype(BF16), after)
    high = jnp.floor(begin_row * (1.0 / 128.0))
    line = iota((16, PEERS), 0)
    tail = jnp.where(line == 0, high, jnp.where(line == 1, begin_row - 128.0 * high, 0.0))
    got_ref[: NF * SLOTS, :] = acc_ref[...].astype(BF16)
    got_ref[NF * SLOTS :, :] = tail.astype(BF16)
    slot = iota((SLOTS, STEP), 0).astype(F32)
    lane = iota((PEERS, STEP), 1).astype(F32)
    for c in range(ROWS // STEP):
        tile = lane + float(c * STEP)
        p = as_bf16((tile >= begin) & (tile < end))
        p_ref[:, c * STEP : (c + 1) * STEP] = p
        g = dot(got_ref[...], p)
        place = tile[:1, :] - (128.0 * g[NF * SLOTS : NF * SLOTS + 1, :] + g[NF * SLOTS + 1 : NF * SLOTS + 2, :])
        q = slot == place
        q_ref[:, c * STEP : (c + 1) * STEP] = as_bf16(q)
        for f in range(NF):
            value = jnp.sum(jnp.where(q, g[f * SLOTS : (f + 1) * SLOTS, :], 0.0), axis=0, keepdims=True)
            field_ref[f, 2 * c : 2 * c + 1, :] = value[:, :128]
            field_ref[f, 2 * c + 1 : 2 * c + 2, :] = value[:, 128:]

    table = jnp.concatenate([table_ref[...], jnp.zeros((4, 128 - NPFT), F32)], axis=1)
    single_t = jnp.sqrt(1.0 - (0.1 + 0.3 * table[0:1]))
    reflect_t = (1.0 - single_t) / (1.0 + single_t)
    vcmax_t = 0.5 + 1.5 * table[1:2]
    slope_t = 3.0 + 6.0 * table[2:3]
    kroot_t = 0.05 + 0.5 * table[3:4]
    level = iota((16, 128), 0)
    roots_t = jnp.where(level < LEVELS, jnp.exp(-kroot_t * level.astype(F32)), 0.0)
    roots_t = 0.05 * (roots_t / jnp.sum(roots_t, axis=0, keepdims=True))
    kinds = type_ref[...]

    def look(row):
        return jnp.take_along_axis(jnp.broadcast_to(row, (LINES, 128)), kinds, axis=1, mode="promise_in_bounds")

    single = look(single_t)
    reflect_h = look(reflect_t)
    vcmax = look(vcmax_t)
    slope = look(slope_t)
    leaf = leaf_ref[...]
    swdir = 2.0 * field_ref[0]
    swdif = field_ref[1]
    tair = field_ref[2] - 0.5
    vapour = 0.2 + field_ref[3]
    carbon = 0.8 + 0.4 * field_ref[4]
    coszen = 0.1 + 0.9 * field_ref[5]
    wind_speed = 0.5 + 2.0 * field_ref[6]
    extinct = 0.5 / coszen
    reflect_b = 2.0 * extinct * reflect_h / (1.0 + extinct)
    light = sunlit_ref[...].astype(F32) * (
        (1.0 - reflect_b) * swdir * (1.0 - jnp.exp(-extinct * single * leaf))
        + (1.0 - reflect_h) * swdif * (1.0 - jnp.exp(-0.8 * single * leaf))
    )
    electrons = 0.3 * light
    compensation = 0.08 * (1.0 + 0.3 * tair)
    capacity_t = vcmax * jnp.exp(0.5 * tair)
    internal = 0.7 * carbon
    for repeat in range(ITERS):
        limit = internal - compensation
        carboxyl = capacity_t * limit / (internal + 0.6)
        ribulose = electrons * limit / (4.0 * internal + 8.0 * compensation)
        assim = carboxyl * ribulose / (carboxyl + ribulose)
        conduct = 0.05 + slope * assim / carbon
        internal = carbon - 1.6 * assim / conduct
    transpire = conduct * vapour
    flux_ref[0] = assim
    flux_ref[1] = transpire
    flux_ref[2] = 0.5 * wind_speed * (0.2 * light - 0.5 * transpire)

    top = iota((16, 128), 0) == 0
    for j in range(LINES):
        kind = jnp.broadcast_to(type_ref[j : j + 1, :], (16, 128))
        draw = jnp.take_along_axis(roots_t, kind, axis=1, mode="promise_in_bounds")
        draw = (draw * flux_ref[1, j : j + 1, :])[:LEVELS]
        theta = soil_ref[:, 128 * j : 128 * (j + 1)]
        theta = theta + jnp.where(top, 0.1 * field_ref[7, j : j + 1, :], 0.0)[:LEVELS]
        for repeat in range(SOILP):
            above = jnp.concatenate([theta[:1], theta[:-1]], axis=0)
            under = jnp.concatenate([theta[1:], theta[-1:]], axis=0)
            theta = theta + 0.25 * (above + under - 2.0 * theta) - draw
        after_ref[:, 128 * j : 128 * (j + 1)] = theta
        flux_ref[3, j : j + 1, :] = 0.5 * theta[LEVELS - 1 :, :]

    for g in range(ROWS // WIDE):
        for k in range(WIDE // 128):
            j = g * (WIDE // 128) + k
            hot = q_ref[:, 128 * j : 128 * (j + 1)]
            for f in range(NOUT):
                w_ref[f * SLOTS : (f + 1) * SLOTS, 128 * k : 128 * (k + 1)] = spread(hot, flux_ref[f, j : j + 1, :])
        part = dot_nt(w_ref[...], p_ref[:, g * WIDE : (g + 1) * WIDE])
        if g == 0:
            acc_ref[: NOUT * SLOTS, :] = part
        else:
            acc_ref[: NOUT * SLOTS, :] += part
    for i in range(3):
        msg_ref[pl.ds(i, PEERS, stride=8), :] = acc_ref[128 * i : 128 * (i + 1), :].T


def gather_kernel(recv_ref, owner_ref, rank_ref, area_ref, column_ref, atm_ref, acc_ref):
    unfold(recv_ref, acc_ref, 3)
    got = acc_ref[: NOUT * SLOTS, :].astype(BF16)
    ids = iota((PEERS, 128), 0)
    slot = iota((SLOTS, 128), 0).astype(F32)
    for b in range(ROWS // BROWS):
        weights, targets = [], []
        for k in range(BROWS // STEP):
            c = b * (BROWS // STEP) + k
            a = jnp.concatenate(
                [as_bf16(ids == owner_ref[j : j + 1, :]) for j in (2 * c, 2 * c + 1)], axis=1
            )
            g = dot(got, a)
            q = jnp.concatenate([slot == rank_ref[j : j + 1, :] for j in (2 * c, 2 * c + 1)], axis=1)
            scale = jnp.concatenate([area_ref[j : j + 1, :] for j in (2 * c, 2 * c + 1)], axis=1)
            rows = [
                jnp.sum(jnp.where(q, g[f * SLOTS : (f + 1) * SLOTS, :], 0.0), axis=0, keepdims=True) * scale
                for f in range(NOUT)
            ]
            weights.append(jnp.concatenate(rows, axis=0))
            targets += [as_bf16(ids == column_ref[j : j + 1, :]) for j in (2 * c, 2 * c + 1)]
        weight = jnp.concatenate(weights, axis=1)
        high = weight.astype(BF16).astype(F32)
        both = jnp.concatenate([high, weight - high], axis=0).astype(BF16)
        total = dot_nt(both, jnp.concatenate(targets, axis=1))
        atm_ref[:, BCOLS * b : BCOLS * (b + 1)] = total[:NOUT] + total[NOUT:]


VMEM_LIMIT = 48 * 1024 * 1024


def local_call(kernel, outs, scratch, name):
    return pl.pallas_call(
        kernel,
        out_shape=outs,
        scratch_shapes=scratch,
        compiler_params=pltpu.CompilerParams(vmem_limit_bytes=VMEM_LIMIT),
        name=name,
    )


def shape(dims, dtype=F32):
    return jax.ShapeDtypeStruct(dims, dtype)


def body(cols, forcing, owner, column, area, sunlit, plant_type, leaf_area, soil_water, pft_table):
    lines = lambda x: x.reshape(LINES, 128)
    owner = lines(owner)
    message, rank = local_call(
        pack_kernel,
        (shape((PEERS * 8, 128)), shape((LINES, 128))),
        [
            pltpu.VMEM((PEERS, ROWS), BF16),
            pltpu.VMEM((NF * SLOTS + 16, WIDE), BF16),
            pltpu.VMEM((NF * SLOTS + 16, PEERS), F32),
        ],
        "pack",
    )(owner, forcing)
    arrived = exchange(message, NF * SLOTS // 128, cols, 1)
    reply, soil_after = local_call(
        land_kernel,
        (shape((PEERS * 8, 128)), shape((LEVELS, ROWS))),
        [
            pltpu.VMEM((NF * SLOTS + 16, PEERS), BF16),
            pltpu.VMEM((PEERS, ROWS), BF16),
            pltpu.VMEM((SLOTS, ROWS), BF16),
            pltpu.VMEM((NF, LINES, 128), F32),
            pltpu.VMEM((NOUT, LINES, 128), F32),
            pltpu.VMEM((NOUT * SLOTS, WIDE), BF16),
            pltpu.VMEM((NF * SLOTS, PEERS), F32),
        ],
        "land",
    )(arrived, lines(sunlit), lines(plant_type), lines(leaf_area), soil_water, pft_table)
    returned = exchange(reply, 3, cols, 2)
    atm_flux = local_call(
        gather_kernel,
        shape((NOUT, ROWS // BROWS * BCOLS)),
        [pltpu.VMEM((384, PEERS), F32)],
        "gather",
    )(returned, owner, rank, lines(area), lines(column))
    return (atm_flux, soil_after)


def solution(mesh):
    spec = P(("row", "col"))
    wide = P(None, ("row", "col"))
    return jax.shard_map(
        functools.partial(body, mesh.shape["col"]),
        mesh=mesh,
        in_specs=(wide, spec, spec, spec, spec, spec, spec, wide, P()),
        out_specs=(wide, wide),
        check_vma=False,
    )
```

time: 403 us -> 59.4 us (0.15)
  local copies, waits for them, and re-layouts: 332 us -> 5.34 us
  Pallas kernels: 0 us -> 53.1 us
  starting transfers between devices: 26.3 us -> 0 us
  other arithmetic: 24.4 us -> 0 us
  waiting for transfers between devices: 14.6 us -> 0 us
    gather x8 -> x0, local copies, waits for them, and re-layouts: 287 us -> none  [the longest x1 56.8 us: body(): order[send_pick].reshape(-1)]
    pallas_call x0 -> x5, Pallas kernels: none -> 53.1 us  [the longest x2 32.9 us: exchange(): pl.pallas_call(functools.partial(exchange_kernel, lines, cols), out_shape...]
    scatter x1 -> x0, local copies, waits for them, and re-layouts: 31 us -> none  [body(): row_place = jnp.zeros((rows_here,), jnp.int32).at[order].set(sorted_pos)]
    all_to_all x3 -> x0, starting transfers between devices: 26.3 us -> none  [the longest x1 11.5 us: body(): lax.all_to_all(count_note, ('row', 'col'), split_axis=1, concat_axis=1, t...]
    all_to_all x3 -> x0, waiting for transfers between devices: 14.6 us -> none  [the longest x1 9.8 us: body(): lax.all_to_all(homeward, ('row', 'col'), split_axis=1, concat_axis=1, til...]
    sort x1 -> x0, other arithmetic: 7.52 us -> none  [body(): order = jnp.argsort(owner, stable=True)]
    reshape x3 -> x0, local copies, waits for them, and re-layouts: 5.26 us -> none  [the longest x1 2.4 us: body(): tile_flux[:, back_pick.reshape(-1)].reshape(NOUT, peer_count, capacity)]
  transfers between devices with their start and end apart: 3 -> 0, of which waited for: 2 -> 0; matrix products, arithmetic and copies ran while one was open for 59% -> 0% of each run, Pallas kernels for 0% -> 0%
where the time goes in v1:
time: 59.4 us; the launch traced here: 59.2 us
  Pallas kernels  53.1 us (89%)
  local copies, waits for them, and re-layouts  5.34 us (9%)
  between operations  0.76 us (1%)
    pallas_call x2, Pallas kernels, exchange(): pl.pallas_call(functools.partial(exchange_kernel, lines, cols), out_shape...  32.9 us
    pallas_call x1, Pallas kernels, body(): local_call(land_kernel, (shape((PEERS * 8, 128)), shape((LEVELS, ROWS))),...  7.82 us
    pallas_call x1, Pallas kernels, body(): local_call(pack_kernel, (shape((PEERS * 8, 128)), shape((LINES, 128))), [...  7.81 us
    unnamed x28, local copies, waits for them, and re-layouts  5.34 us
    pallas_call x1, Pallas kernels, body(): local_call(gather_kernel, shape((NOUT, ROWS // BROWS * BCOLS)), [pltpu.VM...  4.54 us

profile of v1, /device:TPU:1, one launch (start us, length us, event | category | flops | bytes accessed | tf_op | source)
XLA Modules:
  0.0 59.2 jit_solution(7819671973744020839)
XLA Ops:
  0.6 0.0 copy-start.5
  0.6 0.9 %copy-done.5 = bf16[8,8192]{1,0:T(8,128)(2,1)S(1)} copy-done((bf16[8,8192]{1,0:T(8,128)(2,1)S(1)}, bf16[8,8192]{1,0:T(8,128)(2,1)}, u32[]{:S(2)}) %copy-start.5) | copy-done | bytes 131096
  1.5 0.0 copy-start.6
  1.5 0.8 %copy-done.6 = s32[8192]{0:T(1024)S(1)} copy-done((s32[8192]{0:T(1024)S(1)}, s32[8192]{0:T(1024)}, u32[]{:S(2)}) %copy-start.6) | copy-done | bytes 32792
  2.3 7.8 %pack.1 = (f32[1024,128]{1,0:T(8,128)S(1)}, f32[64,128]{1,0:T(8,128)S(1)}) custom-call(s32[64,128]{1,0:T(8,128)S(1)} %bitcast.14, bf16[8,8192]{1,0:T(8,128)(2,1)S(1)} %copy-done.5), custom_call_target="tpu_custom_call" | custom-call | tf_op jit(solution)/shard_map/pack/pallas_call | solution.py:299
  10.1 0.0 copy-start.4
  10.1 0.8 %copy-done.4 = f32[1024,128]{1,0:T(8,128)} copy-done((f32[1024,128]{1,0:T(8,128)}, f32[1024,128]{1,0:T(8,128)S(1)}, u32[]{:S(2)}) %copy-start.4) | copy-done | bytes 524312
  10.9 0.0 copy-start.2
  10.9 0.0 copy-start.8
  10.9 0.0 copy-start.10
  10.9 0.0 copy-start.13
  10.9 19.6 %shard_map.104 = f32[128,8,128]{2,1,0:T(8,128)} custom-call(f32[128,8,128]{2,1,0:T(8,128)} %bitcast.13), custom_call_target="tpu_custom_call" | custom-call | tf_op jit(solution)/shard_map/pallas_call | solution.py:125
  30.5 0.0 copy-done.2
  30.5 0.0 copy-done.8
  30.5 0.0 copy-done.9
  30.6 0.0 copy-done.10
  30.6 0.0 copy-done.13
  30.6 0.0 copy-start
  30.6 1.0 %copy-done = f32[128,8,128]{2,1,0:T(8,128)S(1)} copy-done((f32[128,8,128]{2,1,0:T(8,128)S(1)}, f32[128,8,128]{2,1,0:T(8,128)}, u32[]{:S(2)}) %copy-start) | copy-done | bytes 524312
  31.6 7.8 %land.1 = (f32[1024,128]{1,0:T(8,128)S(1)}, f32[15,8192]{1,0:T(8,128)}) custom-call(f32[1024,128]{1,0:T(8,128)S(1)} %bitcast.10, s32[64,128]{1,0:T(8,128)S(1)} %bitcast.16, s32[64,128]{1,0:T(8,128)S(1)} %bitcast.17, f32[64,128]{1,0:T(8,128)S(1)} %bitcast.18, f32[15,8192]{1,0:T(8,128)S(1)} %copy-done.2, f32[4,16]{1,0:T(4,128)S(1)} %copy-done.13), custom_call_target="tpu_custom_call" | custom-call | tf_op jit(solution)/shard_map/land/pallas_call | solution.py:310
  39.4 0.0 copy-start.3
  39.4 0.8 %copy-done.3 = f32[1024,128]{1,0:T(8,128)} copy-done((f32[1024,128]{1,0:T(8,128)}, f32[1024,128]{1,0:T(8,128)S(1)}, u32[]{:S(2)}) %copy-start.3) | copy-done | bytes 524312
  40.2 0.0 copy-start.7
  40.2 0.0 copy-start.11
  40.2 0.0 copy-start.12
  40.2 13.3 %shard_map.105 = f32[128,8,128]{2,1,0:T(8,128)} custom-call(f32[128,8,128]{2,1,0:T(8,128)} %bitcast.12), custom_call_target="tpu_custom_call" | custom-call | tf_op jit(solution)/shard_map/pallas_call | solution.py:125
  53.5 0.0 copy-done.7
  53.6 0.0 copy-done.11
  53.6 0.0 copy-done.12
  53.6 0.0 copy-start.1
  53.6 1.0 %copy-done.1 = f32[128,8,128]{2,1,0:T(8,128)S(1)} copy-done((f32[128,8,128]{2,1,0:T(8,128)S(1)}, f32[128,8,128]{2,1,0:T(8,128)}, u32[]{:S(2)}) %copy-start.1) | copy-done | bytes 524312
  54.6 4.5 %gather.1 = f32[4,2048]{1,0:T(4,128)} custom-call(f32[1024,128]{1,0:T(8,128)S(1)} %bitcast.11, s32[64,128]{1,0:T(8,128)S(1)} %bitcast.15, f32[64,128]{1,0:T(8,128)S(1)} %get-tuple-element.8.rank_ref, f32[64,128]{1,0:T(8,128)S(1)} %bitcast.19, s32[64,128]{1,0:T(8,128)S(1)} %bitcast.20), custom_call_target="tpu_custom_call" | custom-call | tf_op jit(solution)/shard_map/gather/pallas_call | solution.py:325
  (1 shorter events, 0.0 us)
Async XLA Ops:
  0.6 0.9 %copy-start.5 = (bf16[8,8192]{1,0:T(8,128)(2,1)S(1)}, bf16[8,8192]{1,0:T(8,128)(2,1)}, u32[]{:S(2)}) copy-start(bf16[8,8192]{1,0:T(8,128)(2,1)} %forcing_ref.1) | copy-start | bytes 393220
  1.5 0.8 %copy-start.6 = (s32[8192]{0:T(1024)S(1)}, s32[8192]{0:T(1024)}, u32[]{:S(2)}) copy-start(s32[8192]{0:T(1024)} %param.10) | copy-start | bytes 98308
  10.1 0.8 %copy-start.4 = (f32[1024,128]{1,0:T(8,128)}, f32[1024,128]{1,0:T(8,128)S(1)}, u32[]{:S(2)}) copy-start(f32[1024,128]{1,0:T(8,128)S(1)} %get-tuple-element.6) | copy-start | bytes 1572868
  10.9 19.6 %copy-start.2 = (f32[15,8192]{1,0:T(8,128)S(1)}, f32[15,8192]{1,0:T(8,128)}, u32[]{:S(2)}) copy-start(f32[15,8192]{1,0:T(8,128)} %soil_ref.1) | copy-start | bytes 1474564
  10.9 19.6 %copy-start.8 = (s32[8192]{0:T(1024)S(1)}, s32[8192]{0:T(1024)}, u32[]{:S(2)}) copy-start(s32[8192]{0:T(1024)} %param.13) | copy-start | bytes 98308
  10.9 19.6 %copy-start.9 = (s32[8192]{0:T(1024)S(1)}, s32[8192]{0:T(1024)}, u32[]{:S(2)}) copy-start(s32[8192]{0:T(1024)} %param.14) | copy-start | bytes 98308
  10.9 19.6 %copy-start.10 = (f32[8192]{0:T(1024)S(1)}, f32[8192]{0:T(1024)}, u32[]{:S(2)}) copy-start(f32[8192]{0:T(1024)} %param.15) | copy-start | bytes 98308
  10.9 19.7 %copy-start.13 = (f32[4,16]{1,0:T(4,128)S(1)}, f32[4,16]{1,0:T(4,128)}, u32[]{:S(2)}) copy-start(f32[4,16]{1,0:T(4,128)} %table_ref.1) | copy-start | bytes 772
  30.6 1.0 %copy-start = (f32[128,8,128]{2,1,0:T(8,128)S(1)}, f32[128,8,128]{2,1,0:T(8,128)}, u32[]{:S(2)}) copy-start(f32[128,8,128]{2,1,0:T(8,128)} %shard_map.104) | copy-start | bytes 1572868
  39.4 0.8 %copy-start.3 = (f32[1024,128]{1,0:T(8,128)}, f32[1024,128]{1,0:T(8,128)S(1)}, u32[]{:S(2)}) copy-start(f32[1024,128]{1,0:T(8,128)S(1)} %get-tuple-element.7) | copy-start | bytes 1572868
  40.2 13.3 %copy-start.7 = (s32[8192]{0:T(1024)S(1)}, s32[8192]{0:T(1024)}, u32[]{:S(2)}) copy-start(s32[8192]{0:T(1024)} %param.10) | copy-start | bytes 98308
  40.2 13.3 %copy-start.11 = (f32[8192]{0:T(1024)S(1)}, f32[8192]{0:T(1024)}, u32[]{:S(2)}) copy-start(f32[8192]{0:T(1024)} %param.12) | copy-start | bytes 98308
  40.2 13.3 %copy-start.12 = (s32[8192]{0:T(1024)S(1)}, s32[8192]{0:T(1024)}, u32[]{:S(2)}) copy-start(s32[8192]{0:T(1024)} %param.11) | copy-start | bytes 98308
  53.6 1.0 %copy-start.1 = (f32[128,8,128]{2,1,0:T(8,128)S(1)}, f32[128,8,128]{2,1,0:T(8,128)}, u32[]{:S(2)}) copy-start(f32[128,8,128]{2,1,0:T(8,128)} %shard_map.105) | copy-start | bytes 1572868

commit v2 on v1

--- a/solution.py
+++ b/solution.py
@@ -1,5 +1,3 @@
-import functools
-
 import jax
 import jax.numpy as jnp
 from jax import lax
@@ -85,51 +83,57 @@
         msg_ref[pl.ds(i, PEERS, stride=8), :] = acc_ref[128 * i : 128 * (i + 1), :].T
 
 
-def exchange_kernel(lines, cols, in_ref, out_ref, send_sem, recv_sem):
-    me = lax.axis_index("row") * cols + lax.axis_index("col")
+def hops(step):
+    return min(step, 4 - step)
+
+
+OFFSETS = sorted(
+    [(y, k, x, z) for y in range(4) for k in range(2) for x in range(4) for z in range(4)][1:],
+    key=lambda o: -(3 * (hops(o[0]) + hops(o[2]) + hops(o[3])) + o[1]),
+)
+
+
+def place():
+    row, col = lax.axis_index("row"), lax.axis_index("col")
+    return row // 2, lax.rem(row, 2), col // 4, lax.rem(col, 4)
+
+
+def neighbour(here, offset):
+    y, k, x, z = (lax.rem(a + b, n) for a, b, n in zip(here, offset, (4, 2, 4, 4)))
+    return y * 2 + k, x * 4 + z
+
+
+def greet(here):
     barrier = pltpu.get_barrier_semaphore()
-
-    def place(p):
-        to = lax.rem(me + p, PEERS)
-        return to, (to // cols, lax.rem(to, cols))
-
-    def greet(p, carry):
-        pl.semaphore_signal(barrier, inc=1, device_id=place(p)[1], device_id_type=MESH)
-        return carry
-
-    lax.fori_loop(1, PEERS, greet, 0)
-    pl.semaphore_wait(barrier, PEERS - 1)
-    own = pltpu.make_async_copy(in_ref.at[me, :lines], out_ref.at[me, :lines], recv_sem)
-    own.start()
-
-    def send(p, carry):
-        to, device = place(p)
+    for offset in OFFSETS:
+        pl.semaphore_signal(barrier, inc=1, device_id=neighbour(here, offset), device_id_type=MESH)
+
+
+def block(ref, index, lines):
+    return ref.at[pl.ds(pl.multiple_of(index * 8, 8), lines), :]
+
+
+def send_all(here, msg_ref, got_ref, lines, send_sem, recv_sem):
+    row, col = neighbour(here, (0, 0, 0, 0))
+    me = row * 16 + col
+    for offset in OFFSETS:
+        row, col = neighbour(here, offset)
         pltpu.make_async_remote_copy(
-            src_ref=in_ref.at[to, :lines],
-            dst_ref=out_ref.at[me, :lines],
+            src_ref=block(msg_ref, row * 16 + col, lines),
+            dst_ref=block(got_ref, me, lines),
             send_sem=send_sem,
             recv_sem=recv_sem,
-            device_id=device,
+            device_id=(row, col),
             device_id_type=MESH,
         ).start()
-        return carry
-
-    lax.fori_loop(1, PEERS, send, 0)
-    sent = in_ref.at[: PEERS - 1, :lines]
+    pltpu.make_async_copy(block(msg_ref, me, lines), block(got_ref, me, lines), recv_sem).start()
+
+
+def await_all(msg_ref, got_ref, lines, send_sem, recv_sem):
+    sent = msg_ref.at[: (PEERS - 1) * lines, :]
     pltpu.make_async_copy(sent, sent, send_sem).wait()
-    got = out_ref.at[:, :lines]
+    got = got_ref.at[: PEERS * lines, :]
     pltpu.make_async_copy(got, got, recv_sem).wait()
-
-
-def exchange(message, lines, cols, ident):
-    return pl.pallas_call(
-        functools.partial(exchange_kernel, lines, cols),
-        out_shape=jax.ShapeDtypeStruct((PEERS, 8, 128), F32),
-        in_specs=[pl.BlockSpec(memory_space=pl.ANY)],
-        out_specs=pl.BlockSpec(memory_space=pl.ANY),
-        scratch_shapes=[pltpu.SemaphoreType.DMA, pltpu.SemaphoreType.DMA],
-        compiler_params=pltpu.CompilerParams(collective_id=ident, has_side_effects=True),
-    )(message.reshape(PEERS, 8, 128)).reshape(PEERS * 8, 128)
 
 
 def unfold(recv_ref, out_ref, lines):
@@ -154,7 +158,7 @@
     high = jnp.floor(begin_row * (1.0 / 128.0))
     line = iota((16, PEERS), 0)
     tail = jnp.where(line == 0, high, jnp.where(line == 1, begin_row - 128.0 * high, 0.0))
-    got_ref[: NF * SLOTS, :] = acc_ref[...].astype(BF16)
+    got_ref[: NF * SLOTS, :] = acc_ref[: NF * SLOTS, :].astype(BF16)
     got_ref[NF * SLOTS :, :] = tail.astype(BF16)
     slot = iota((SLOTS, STEP), 0).astype(F32)
     lane = iota((PEERS, STEP), 1).astype(F32)
@@ -239,7 +243,7 @@
             hot = q_ref[:, 128 * j : 128 * (j + 1)]
             for f in range(NOUT):
                 w_ref[f * SLOTS : (f + 1) * SLOTS, 128 * k : 128 * (k + 1)] = spread(hot, flux_ref[f, j : j + 1, :])
-        part = dot_nt(w_ref[...], p_ref[:, g * WIDE : (g + 1) * WIDE])
+        part = dot_nt(w_ref[: NOUT * SLOTS, :], p_ref[:, g * WIDE : (g + 1) * WIDE])
         if g == 0:
             acc_ref[: NOUT * SLOTS, :] = part
         else:
@@ -276,66 +280,92 @@
         atm_ref[:, BCOLS * b : BCOLS * (b + 1)] = total[:NOUT] + total[NOUT:]
 
 
-VMEM_LIMIT = 48 * 1024 * 1024
-
-
-def local_call(kernel, outs, scratch, name):
+VMEM_LIMIT = 56 * 1024 * 1024
+
+
+def step_kernel(
+    owner_hbm, forcing_hbm, sunlit_hbm, type_hbm, leaf_hbm, soil_hbm, table_hbm, area_hbm, column_hbm,
+    atm_ref, after_ref,
+    owner_ref, forcing_ref, sunlit_ref, type_ref, leaf_ref, soil_ref, table_ref, area_ref, column_ref,
+    in_sem, send_sem, recv_sem,
+    msg_ref, got_ref, reply_ref, home_ref,
+    rank_ref, at_ref, w_ref, acc_ref, lhs_ref, p_ref, q_ref, field_ref, flux_ref,
+):
+    copies = [
+        pltpu.make_async_copy(a, b, in_sem.at[i])
+        for i, (a, b) in enumerate(
+            (
+                (owner_hbm, owner_ref), (forcing_hbm, forcing_ref), (sunlit_hbm, sunlit_ref),
+                (type_hbm, type_ref), (leaf_hbm, leaf_ref), (soil_hbm, soil_ref), (table_hbm, table_ref),
+                (area_hbm, area_ref), (column_hbm, column_ref),
+            )
+        )
+    ]
+    for copy in copies:
+        copy.start()
+    here = place()
+    greet(here)
+    copies[0].wait()
+    copies[1].wait()
+    pack_kernel(owner_ref, forcing_ref, msg_ref, rank_ref, at_ref, w_ref, acc_ref)
+    pl.semaphore_wait(pltpu.get_barrier_semaphore(), PEERS - 1)
+    send_all(here, msg_ref, got_ref, 5, send_sem.at[0], recv_sem.at[0])
+    for copy in copies[2:]:
+        copy.wait()
+    await_all(msg_ref, got_ref, 5, send_sem.at[0], recv_sem.at[0])
+    land_kernel(
+        got_ref, sunlit_ref, type_ref, leaf_ref, soil_ref, table_ref,
+        reply_ref, after_ref,
+        lhs_ref, p_ref, q_ref, field_ref, flux_ref, w_ref, acc_ref,
+    )
+    send_all(here, reply_ref, home_ref, 3, send_sem.at[1], recv_sem.at[1])
+    await_all(reply_ref, home_ref, 3, send_sem.at[1], recv_sem.at[1])
+    gather_kernel(home_ref, owner_ref, rank_ref, area_ref, column_ref, atm_ref, acc_ref)
+
+
+def body(forcing, owner, column, area, sunlit, plant_type, leaf_area, soil_water, pft_table):
+    lines = lambda x: x.reshape(LINES, 128)
+    i32 = jnp.int32
+    flat = lambda dtype: pltpu.VMEM((LINES, 128), dtype)
+    message = pltpu.VMEM((PEERS * 8, 128), F32)
     return pl.pallas_call(
-        kernel,
-        out_shape=outs,
-        scratch_shapes=scratch,
-        compiler_params=pltpu.CompilerParams(vmem_limit_bytes=VMEM_LIMIT),
-        name=name,
-    )
-
-
-def shape(dims, dtype=F32):
-    return jax.ShapeDtypeStruct(dims, dtype)
-
-
-def body(cols, forcing, owner, column, area, sunlit, plant_type, leaf_area, soil_water, pft_table):
-    lines = lambda x: x.reshape(LINES, 128)
-    owner = lines(owner)
-    message, rank = local_call(
-        pack_kernel,
-        (shape((PEERS * 8, 128)), shape((LINES, 128))),
-        [
+        step_kernel,
+        out_shape=(
+            jax.ShapeDtypeStruct((NOUT, ROWS // BROWS * BCOLS), F32),
+            jax.ShapeDtypeStruct((LEVELS, ROWS), F32),
+        ),
+        in_specs=[pl.BlockSpec(memory_space=pl.ANY)] * 9,
+        out_specs=(pl.BlockSpec(memory_space=pltpu.VMEM),) * 2,
+        scratch_shapes=[
+            flat(i32), pltpu.VMEM((NF, ROWS), BF16), flat(i32), flat(i32), flat(F32),
+            pltpu.VMEM((LEVELS, ROWS), F32), pltpu.VMEM((4, NPFT), F32), flat(F32), flat(i32),
+            pltpu.SemaphoreType.DMA((9,)), pltpu.SemaphoreType.DMA((2,)), pltpu.SemaphoreType.DMA((2,)),
+            message, message, message, message,
+            flat(F32),
             pltpu.VMEM((PEERS, ROWS), BF16),
             pltpu.VMEM((NF * SLOTS + 16, WIDE), BF16),
             pltpu.VMEM((NF * SLOTS + 16, PEERS), F32),
-        ],
-        "pack",
-    )(owner, forcing)
-    arrived = exchange(message, NF * SLOTS // 128, cols, 1)
-    reply, soil_after = local_call(
-        land_kernel,
-        (shape((PEERS * 8, 128)), shape((LEVELS, ROWS))),
-        [
             pltpu.VMEM((NF * SLOTS + 16, PEERS), BF16),
             pltpu.VMEM((PEERS, ROWS), BF16),
             pltpu.VMEM((SLOTS, ROWS), BF16),
             pltpu.VMEM((NF, LINES, 128), F32),
             pltpu.VMEM((NOUT, LINES, 128), F32),
-            pltpu.VMEM((NOUT * SLOTS, WIDE), BF16),
-            pltpu.VMEM((NF * SLOTS, PEERS), F32),
         ],
-        "land",
-    )(arrived, lines(sunlit), lines(plant_type), lines(leaf_area), soil_water, pft_table)
-    returned = exchange(reply, 3, cols, 2)
-    atm_flux = local_call(
-        gather_kernel,
-        shape((NOUT, ROWS // BROWS * BCOLS)),
-        [pltpu.VMEM((384, PEERS), F32)],
-        "gather",
-    )(returned, owner, rank, lines(area), lines(column))
-    return (atm_flux, soil_after)
+        compiler_params=pltpu.CompilerParams(
+            collective_id=1, has_side_effects=True, vmem_limit_bytes=VMEM_LIMIT
+        ),
+        name="step",
+    )(
+        lines(owner), forcing, lines(sunlit), lines(plant_type), lines(leaf_area), soil_water, pft_table,
+        lines(area), lines(column),
+    )
 
 
 def solution(mesh):
     spec = P(("row", "col"))
     wide = P(None, ("row", "col"))
     return jax.shard_map(
-        functools.partial(body, mesh.shape["col"]),
+        body,
         mesh=mesh,
         in_specs=(wide, spec, spec, spec, spec, spec, spec, wide, P()),
         out_specs=(wide, wide),

time: 59.4 us -> 47.6 us (0.80)
  Pallas kernels: 53.1 us -> 43.5 us
  local copies, waits for them, and re-layouts: 5.34 us -> 3.24 us
    pallas_call x5 -> x1, Pallas kernels: 53.1 us -> 43.5 us  [body(): pl.pallas_call(step_kernel, out_shape=(jax.ShapeDtypeStruct((NOUT, ROWS /...]
    unnamed x28 -> x2, local copies, waits for them, and re-layouts: 5.34 us -> 3.24 us
where the time goes in v2:
time: 47.6 us; the launch traced here: 47.4 us
  Pallas kernels  43.5 us (91%)
  local copies, waits for them, and re-layouts  3.24 us (7%)
  between operations  0.64 us (1%)
    pallas_call x1, Pallas kernels, body(): pl.pallas_call(step_kernel, out_shape=(jax.ShapeDtypeStruct((NOUT, ROWS /...  43.5 us
    unnamed x2, local copies, waits for them, and re-layouts  3.24 us

profile of v2, /device:TPU:1, one launch (start us, length us, event | category | flops | bytes accessed | tf_op | source)
XLA Modules:
  0.0 47.4 jit_solution(13079509603869939803)
XLA Ops:
  0.6 43.5 %step.1 = (f32[4,2048]{1,0:T(4,128)}, f32[15,8192]{1,0:T(8,128)}) custom-call(s32[64,128]{1,0:T(8,128)} %bitcast.6, bf16[8,8192]{1,0:T(8,128)(2,1)} %forcing_hbm.1, s32[64,128]{1,0:T(8,128)} %bitcast.7, s32[64,128]{1,0:T(8,128)} %bitcast.8, f32[64,128]{1,0:T(8,128)} %bitcast.9, f32[15,8192]{1,0:T(8,128)} %soil_hbm.1, f32[4,16]{1,0:T(4,128)} %table_hbm.1, ...), custom_call_target="tpu_custom_call" | custom-call | tf_op jit(solution)/shard_map/step/pallas_call | solution.py:331
  44.1 1.4 %copy.13 = f32[4,2048]{1,0:T(4,128)} copy(f32[4,2048]{1,0:T(4,128)} %get-tuple-element.4) | data formatting | bytes 65536
  45.5 1.9 %copy.14 = f32[15,8192]{1,0:T(8,128)} copy(f32[15,8192]{1,0:T(8,128)} %get-tuple-element.5) | data formatting | bytes 983040

commit v3 on v2

v3 whole, which is shorter than its diff:
```python
import jax
import jax.numpy as jnp
from jax import lax
from jax.experimental import pallas as pl
from jax.experimental.pallas import tpu as pltpu
from jax.sharding import PartitionSpec as P

NF = 8
NOUT = 4
NPFT = 16
LEVELS = 15
ITERS = 4
SOILP = 4
BROWS = 512
BCOLS = 128
PEERS = 128
ROWS = 8192
LINES = ROWS // 128
SLOTS = 80
QUADS = SLOTS // 4
STEP = 256
CHUNKS = ROWS // STEP
HALF = 2 * QUADS * NF
WINDOW = 64
SENT = NF * SLOTS // 128
BACK = 3
MESH = pl.DeviceIdType.MESH
F32 = jnp.float32
BF16 = jnp.bfloat16
NT = (((1,), (1,)), ((), ()))
VMEM_LIMIT = 56 * 1024 * 1024


def iota(shape, dim):
    return lax.broadcasted_iota(jnp.int32, shape, dim)


def as_bf16(mask):
    return jnp.where(mask, 1.0, 0.0).astype(BF16)


def dot(a, b):
    return jnp.dot(a, b, preferred_element_type=F32)


def dot_nt(a, b):
    return lax.dot_general(a, b, NT, preferred_element_type=F32)


def times_row(hot, row):
    rows, width = hot.shape
    tile = jnp.broadcast_to(row, (16, width)).astype(BF16)
    return (hot.reshape(rows // 16, 16, width) * tile[None]).reshape(rows, width)


def two_lines(ref, c):
    return jnp.concatenate([ref[2 * c : 2 * c + 1, :], ref[2 * c + 1 : 2 * c + 2, :]], axis=1)


def hops(step):
    return min(step, 4 - step)


OFFSETS = sorted(
    [(y, k, x, z) for y in range(4) for k in range(2) for x in range(4) for z in range(4)][1:],
    key=lambda o: -(3 * (hops(o[0]) + hops(o[2]) + hops(o[3])) + o[1]),
)


def place():
    row, col = lax.axis_index("row"), lax.axis_index("col")
    return row // 2, lax.rem(row, 2), col // 4, lax.rem(col, 4)


def neighbour(here, offset):
    y, k, x, z = (lax.rem(a + b, n) for a, b, n in zip(here, offset, (4, 2, 4, 4)))
    return y * 2 + k, x * 4 + z


def greet(here):
    barrier = pltpu.get_barrier_semaphore()
    for offset in OFFSETS:
        pl.semaphore_signal(barrier, inc=1, device_id=neighbour(here, offset), device_id_type=MESH)


def block(ref, index, lines):
    return ref.at[pl.ds(pl.multiple_of(index * 8, 8), lines), :]


def send_all(here, msg_ref, got_ref, lines, send_sem, recv_sem):
    row, col = neighbour(here, (0, 0, 0, 0))
    me = row * 16 + col
    for offset in OFFSETS:
        row, col = neighbour(here, offset)
        pltpu.make_async_remote_copy(
            src_ref=block(msg_ref, row * 16 + col, lines),
            dst_ref=block(got_ref, me, lines),
            send_sem=send_sem,
            recv_sem=recv_sem,
            device_id=(row, col),
            device_id_type=MESH,
        ).start()
    pltpu.make_async_copy(block(msg_ref, me, lines), block(got_ref, me, lines), recv_sem).start()


def await_all(msg_ref, got_ref, lines, send_sem, recv_sem):
    sent = msg_ref.at[: (PEERS - 1) * lines, :]
    pltpu.make_async_copy(sent, sent, send_sem).wait()
    got = got_ref.at[: PEERS * lines, :]
    pltpu.make_async_copy(got, got, recv_sem).wait()


def fold(values, msg_ref, lines):
    for i in range(lines):
        msg_ref[pl.ds(i, PEERS, stride=8), :] = values[128 * i : 128 * (i + 1), :].T


def unfold(got_ref, lines):
    return jnp.concatenate([got_ref[pl.ds(i, PEERS, stride=8), :].T for i in range(lines)], axis=0)


def pack(owner_ref, forcing_ref, msg_ref, pair_ref, a_ref, split_ref, w_ref):
    ids = iota((PEERS, 128), 0)
    for j in range(LINES):
        a_ref[:, 128 * j : 128 * (j + 1)] = as_bf16(ids == owner_ref[j : j + 1, :])
    upto = as_bf16(iota((STEP, STEP), 0) <= iota((STEP, STEP), 1))
    base = jnp.zeros((PEERS, 1), F32)
    for c in range(CHUNKS):
        a = a_ref[:, c * STEP : (c + 1) * STEP]
        seen = dot(a, upto)
        mine = (seen + base).astype(BF16) * a
        base = base + seen[:, STEP - 1 :]
        mine = mine.reshape(PEERS // 16, 16, STEP)
        total = mine[0]
        for i in range(1, PEERS // 16):
            total = total + mine[i]
        rank = jnp.sum(total.astype(F32), axis=0, keepdims=True) - 1.0
        pair = jnp.floor(rank * 0.5)
        odd = rank - 2.0 * pair
        pair_ref[2 * c : 2 * c + 1, :] = pair[:, :128]
        pair_ref[2 * c + 1 : 2 * c + 2, :] = pair[:, 128:]
        split_ref[:PEERS, c * STEP : (c + 1) * STEP] = times_row(a, 1.0 - odd)
        split_ref[PEERS:, c * STEP : (c + 1) * STEP] = times_row(a, odd)
    line = iota((16, STEP), 0)
    for c in range(CHUNKS):
        pair = jnp.broadcast_to(two_lines(pair_ref, c), (16, STEP)).astype(BF16)
        x = forcing_ref[:, c * STEP : (c + 1) * STEP].astype(F32)
        x = jnp.concatenate([x, x], axis=0).astype(BF16)
        for k in range(2 * QUADS // 2):
            label = 2 * (2 * (k % (QUADS // 2)) + line // 8) + k // (QUADS // 2)
            hit = label.astype(F32).astype(BF16) == pair
            w_ref[16 * k : 16 * (k + 1), c * STEP : (c + 1) * STEP] = jnp.where(hit, x, jnp.zeros((), BF16))
    w_ref[HALF:, :] = jnp.ones((16, ROWS), BF16)
    got = dot_nt(w_ref[...], split_ref[...])
    counts = got[HALF : HALF + 1, :PEERS] + got[HALF : HALF + 1, PEERS:]
    line = iota((HALF, PEERS), 0)
    label = 4 * (lax.rem(line, HALF // 2) // NF) + 2 * (line // (HALF // 2))
    values = [
        jnp.where((label + odd).astype(F32) < counts, got[:HALF, PEERS * odd : PEERS * (odd + 1)], -1.0)
        for odd in range(2)
    ]
    fold(jnp.concatenate(values, axis=0), msg_ref, SENT)


def look(row, kinds):
    return jnp.take_along_axis(jnp.broadcast_to(row, kinds.shape), kinds, axis=1, mode="promise_in_bounds")


def prepare(sunlit_ref, type_ref, leaf_ref, table_ref, early_ref, draw_ref):
    table = jnp.concatenate([table_ref[...], jnp.zeros((4, 128 - NPFT), F32)], axis=1)
    single_t = jnp.sqrt(1.0 - (0.1 + 0.3 * table[0:1]))
    reflect_t = (1.0 - single_t) / (1.0 + single_t)
    kroot_t = 0.05 + 0.5 * table[3:4]
    level = iota((16, 128), 0)
    roots_t = jnp.where(level < LEVELS, jnp.exp(-kroot_t * level.astype(F32)), 0.0)
    roots_t = 0.05 * (roots_t / jnp.sum(roots_t, axis=0, keepdims=True))
    kinds = type_ref[...]
    leaf = leaf_ref[...]
    single = look(single_t, kinds)
    reflect_h = look(reflect_t, kinds)
    lit = sunlit_ref[...].astype(F32)
    early_ref[0] = single * leaf
    early_ref[1] = reflect_h
    early_ref[2] = look(0.5 + 1.5 * table[1:2], kinds)
    early_ref[3] = look(3.0 + 6.0 * table[2:3], kinds)
    early_ref[4] = lit
    early_ref[5] = lit * (1.0 - reflect_h) * (1.0 - jnp.exp(-0.8 * single * leaf))
    for j in range(LINES):
        draw_ref[:, 128 * j : 128 * (j + 1)] = look(roots_t, jnp.broadcast_to(type_ref[j : j + 1, :], (16, 128)))


def window_of(c):
    least = c * STEP // SLOTS
    most = min(PEERS - 1, (PEERS * SLOTS - ROWS + c * STEP + STEP - 1) // SLOTS)
    for w in range(3):
        if 32 * w <= least and most < 32 * w + WINDOW:
            return w
    raise ValueError


def arrange(got_ref, lhs_ref):
    got = unfold(got_ref, SENT)
    valid = jnp.where(got >= 0.0, 1.0 / NF, 0.0)
    counts = jnp.sum(valid, axis=0, keepdims=True)
    part = lambda odd, a: got[HALF * odd + HALF // 2 * a : HALF * odd + HALF // 2 * (a + 1), :]
    low = iota((HALF // 2, 128), 1) < WINDOW
    for a in range(2):
        even, odd = part(0, a), part(1, a)
        for w in range(3):
            left = even if w == 0 else pltpu.roll(even, 128 - 32 * w, 1)
            right = odd if w == 2 else pltpu.roll(odd, 64 - 32 * w, 1)
            lhs_ref[w, :, 128 * a : 128 * (a + 1)] = jnp.where(low, left, right).astype(BF16)
    before = iota((PEERS, PEERS), 1) < iota((PEERS, PEERS), 0)
    upto = iota((PEERS, PEERS), 1) <= iota((PEERS, PEERS), 0)
    ones = jnp.ones((PEERS, STEP), BF16)
    begin = dot(jnp.where(before, counts, 0.0).astype(BF16), ones)
    end = dot(jnp.where(upto, counts, 0.0).astype(BF16), ones)
    return begin, end


def unpack(got_ref, lhs_ref, p_ref, quad_ref, field_ref):
    begin, end = arrange(got_ref, lhs_ref)
    for c in range(CHUNKS):
        w = window_of(c)
        first = begin[32 * w : 32 * w + WINDOW]
        tile = (iota((1, STEP), 1) + c * STEP).astype(F32)
        mine = (tile >= first) & (tile < end[32 * w : 32 * w + WINDOW])
        slot = tile - jnp.sum(jnp.where(mine, first, 0.0), axis=0, keepdims=True)
        quad = jnp.floor(slot * 0.25)
        rest = slot - 4.0 * quad
        quad_ref[2 * c : 2 * c + 1, :] = quad[:, :128]
        quad_ref[2 * c + 1 : 2 * c + 2, :] = quad[:, 128:]
        hot = as_bf16(mine)
        for k in range(4):
            p_ref[WINDOW * k : WINDOW * (k + 1), c * STEP : (c + 1) * STEP] = times_row(
                hot, jnp.where(rest == float(k), 1.0, 0.0)
            )
    for c in range(CHUNKS):
        g = dot(lhs_ref[window_of(c)], p_ref[:, c * STEP : (c + 1) * STEP])
        quad = jnp.broadcast_to(two_lines(quad_ref, c), (NF, STEP))
        value = jnp.zeros((NF, STEP), F32)
        for s in range(QUADS):
            value = value + jnp.where(quad == float(s), g[NF * s : NF * (s + 1), :], 0.0)
        field_ref[NF * 2 * c : NF * (2 * c + 1), :] = value[:, :128]
        field_ref[NF * (2 * c + 1) : NF * (2 * c + 2), :] = value[:, 128:]


def physics(early_ref, field_ref, flux_ref):
    field = lambda f: field_ref[pl.ds(f, LINES, stride=NF), :]
    thick, reflect_h, vcmax, slope, lit, diffuse = (early_ref[i] for i in range(6))
    swdir = 2.0 * field(0)
    tair = field(2) - 0.5
    vapour = 0.2 + field(3)
    carbon = 0.8 + 0.4 * field(4)
    coszen = 0.1 + 0.9 * field(5)
    wind_speed = 0.5 + 2.0 * field(6)
    extinct = 0.5 / coszen
    reflect_b = 2.0 * extinct * reflect_h / (1.0 + extinct)
    light = lit * (1.0 - reflect_b) * swdir * (1.0 - jnp.exp(-extinct * thick)) + diffuse * field(1)
    electrons = 0.3 * light
    compensation = 0.08 * (1.0 + 0.3 * tair)
    capacity_t = vcmax * jnp.exp(0.5 * tair)
    internal = 0.7 * carbon
    for repeat in range(ITERS):
        limit = internal - compensation
        carboxyl = capacity_t * limit / (internal + 0.6)
        ribulose = electrons * limit / (4.0 * internal + 8.0 * compensation)
        assim = carboxyl * ribulose / (carboxyl + ribulose)
        conduct = 0.05 + slope * assim / carbon
        internal = carbon - 1.6 * assim / conduct
    transpire = conduct * vapour
    for f, value in enumerate((assim, transpire, 0.5 * wind_speed * (0.2 * light - 0.5 * transpire))):
        flux_ref[pl.ds(f, LINES, stride=8), :] = value
        flux_ref[pl.ds(f + NOUT, LINES, stride=8), :] = value


def soil_pass(theta, draw, level):
    above = jnp.where(level == 0, theta, pltpu.roll(theta, 1, 0))
    under = jnp.where(level == LEVELS - 1, theta, pltpu.roll(theta, theta.shape[0] - 1, 0))
    return theta + 0.25 * (above + under - 2.0 * theta) - draw


def drain(soil_ref, draw_ref, flux_ref):
    level = iota((8, 128), 0) + 8
    for j in range(LINES):
        lanes = slice(128 * j, 128 * (j + 1))
        draw = draw_ref[8:, lanes] * flux_ref[8 * j + 1 : 8 * j + 2, :]
        theta = jnp.concatenate([soil_ref[8:, lanes], jnp.zeros((1, 128), F32)], axis=0)
        for repeat in range(SOILP):
            theta = soil_pass(theta, draw, level)
        value = 0.5 * theta[LEVELS - 9 : LEVELS - 8, :]
        flux_ref[8 * j + 3 : 8 * j + 4, :] = value
        flux_ref[8 * j + 7 : 8 * j + 8, :] = value


def soil(soil_ref, draw_ref, field_ref, flux_ref):
    level = iota((16, 128), 0)
    for j in range(LINES):
        lanes = slice(128 * j, 128 * (j + 1))
        draw = draw_ref[:, lanes] * flux_ref[8 * j + 1 : 8 * j + 2, :]
        theta = jnp.concatenate([soil_ref[:, lanes], jnp.zeros((1, 128), F32)], axis=0)
        theta = theta + jnp.where(level == 0, 0.1 * field_ref[NF * j + 7 : NF * j + 8, :], 0.0)
        for repeat in range(SOILP):
            theta = soil_pass(theta, draw, level)
        soil_ref[:, lanes] = theta[:LEVELS]


def reply(flux_ref, quad_ref, p_ref, w_ref, msg_ref):
    line = iota((8, 128), 0)
    for j in range(LINES):
        flux = flux_ref[8 * j : 8 * (j + 1), :]
        quad = jnp.broadcast_to(quad_ref[j : j + 1, :], (8, 128))
        parts = [
            jnp.where((2 * k + line // NOUT).astype(F32) == quad, flux, 0.0) for k in range(QUADS // 2)
        ]
        w_ref[: NOUT * QUADS, 128 * j : 128 * (j + 1)] = jnp.concatenate(parts, axis=0).astype(BF16)
    low = iota((NOUT * QUADS, 128), 1)
    total = [[], [], [], []]
    for w in range(3):
        mine = [c for c in range(CHUNKS) if window_of(c) == w]
        lanes = slice(mine[0] * STEP, (mine[-1] + 1) * STEP)
        g = dot_nt(w_ref[: NOUT * QUADS, lanes], p_ref[:, lanes])
        for k in range(4):
            half = g[:, 128 * (k // 2) : 128 * (k // 2 + 1)]
            start = WINDOW * (k % 2)
            half = jnp.where((low >= start) & (low < start + WINDOW), half, 0.0)
            shift = (32 * w - start) % 128
            total[k].append(pltpu.roll(half, shift, 1) if shift else half)
    values = [a + b + c for a, b, c in total]
    values.append(jnp.zeros((BACK * 128 - NOUT * SLOTS, PEERS), F32))
    fold(jnp.concatenate(values, axis=0), msg_ref, BACK)


def targets(column_ref, target_ref):
    ids = iota((BCOLS, 128), 0)
    for j in range(LINES):
        target_ref[:, 128 * j : 128 * (j + 1)] = as_bf16(ids == column_ref[j : j + 1, :])


def gather(home_ref, pair_ref, area_ref, split_ref, target_ref, atm_ref):
    got = unfold(home_ref, BACK)
    rows = NOUT * QUADS
    part = lambda k: got[rows * k : rows * (k + 1), :]
    even = jnp.concatenate([part(0), part(2)], axis=0)
    odd = jnp.concatenate([part(1), part(3)], axis=0)
    lhs = jnp.concatenate([even, odd], axis=1).astype(BF16)
    line = iota((8, STEP), 0)
    for b in range(ROWS // BROWS):
        both = []
        for c in (2 * b, 2 * b + 1):
            g = dot(lhs, split_ref[:, c * STEP : (c + 1) * STEP])
            pair = jnp.broadcast_to(two_lines(pair_ref, c), (8, STEP))
            value = jnp.zeros((8, STEP), F32)
            for k in range(QUADS):
                label = 2 * (2 * (k % (QUADS // 2)) + line // NOUT) + k // (QUADS // 2)
                value = value + jnp.where(label.astype(F32) == pair, g[8 * k : 8 * (k + 1), :], 0.0)
            value = (value + pltpu.roll(value, NOUT, 0)) * two_lines(area_ref, c)
            high = value.astype(BF16).astype(F32)
            both.append(jnp.where(line < NOUT, high, value - high).astype(BF16))
        total = dot_nt(jnp.concatenate(both, axis=1), target_ref[:, b * BROWS : (b + 1) * BROWS])
        atm_ref[:, BCOLS * b : BCOLS * (b + 1)] = total[:NOUT] + total[NOUT:]


def step_kernel(
    owner_hbm, forcing_hbm, sunlit_hbm, type_hbm, leaf_hbm, soil_hbm, table_hbm, area_hbm, column_hbm,
    atm_ref, after_hbm,
    owner_ref, forcing_ref, sunlit_ref, type_ref, leaf_ref, soil_ref, table_ref, area_ref, column_ref,
    in_sem, out_sem, send_sem, recv_sem,
    msg_ref, got_ref, reply_ref, home_ref,
    pair_ref, quad_ref, a_ref, split_ref, w_ref, lhs_ref, p_ref, early_ref, draw_ref, field_ref, flux_ref,
):
    copies = [
        pltpu.make_async_copy(a, b, in_sem.at[i])
        for i, (a, b) in enumerate(
            (
                (owner_hbm, owner_ref), (forcing_hbm, forcing_ref), (sunlit_hbm, sunlit_ref),
                (type_hbm, type_ref), (leaf_hbm, leaf_ref), (soil_hbm, soil_ref),
                (table_hbm, table_ref), (area_hbm, area_ref), (column_hbm, column_ref),
            )
        )
    ]
    for copy in copies:
        copy.start()
    here = place()
    greet(here)
    copies[0].wait()
    copies[1].wait()
    pack(owner_ref, forcing_ref, msg_ref, pair_ref, a_ref, split_ref, w_ref)
    pl.semaphore_wait(pltpu.get_barrier_semaphore(), PEERS - 1)
    send_all(here, msg_ref, got_ref, SENT, send_sem.at[0], recv_sem.at[0])
    for copy in copies[2:]:
        copy.wait()
    prepare(sunlit_ref, type_ref, leaf_ref, table_ref, early_ref, draw_ref)
    await_all(msg_ref, got_ref, SENT, send_sem.at[0], recv_sem.at[0])
    unpack(got_ref, lhs_ref, p_ref, quad_ref, field_ref)
    physics(early_ref, field_ref, flux_ref)
    drain(soil_ref, draw_ref, flux_ref)
    reply(flux_ref, quad_ref, p_ref, w_ref, reply_ref)
    send_all(here, reply_ref, home_ref, BACK, send_sem.at[1], recv_sem.at[1])
    soil(soil_ref, draw_ref, field_ref, flux_ref)
    after = pltpu.make_async_copy(soil_ref, after_hbm, out_sem)
    after.start()
    targets(column_ref, a_ref)
    await_all(reply_ref, home_ref, BACK, send_sem.at[1], recv_sem.at[1])
    gather(home_ref, pair_ref, area_ref, split_ref, a_ref, atm_ref)
    after.wait()


def body(forcing, owner, column, area, sunlit, plant_type, leaf_area, soil_water, pft_table):
    lines = lambda x: x.reshape(LINES, 128)
    i32 = jnp.int32
    flat = lambda dtype: pltpu.VMEM((LINES, 128), dtype)
    message = pltpu.VMEM((PEERS * 8, 128), F32)
    sem = pltpu.SemaphoreType.DMA
    return pl.pallas_call(
        step_kernel,
        out_shape=(
            jax.ShapeDtypeStruct((NOUT, ROWS // BROWS * BCOLS), F32),
            jax.ShapeDtypeStruct((LEVELS, ROWS), F32),
        ),
        in_specs=[pl.BlockSpec(memory_space=pl.ANY)] * 9,
        out_specs=(pl.BlockSpec(memory_space=pltpu.VMEM), pl.BlockSpec(memory_space=pl.ANY)),
        scratch_shapes=[
            flat(i32), pltpu.VMEM((NF, ROWS), BF16), flat(i32), flat(i32), flat(F32),
            pltpu.VMEM((LEVELS, ROWS), F32), pltpu.VMEM((4, NPFT), F32), flat(F32), flat(i32),
            sem((9,)), sem, sem((2,)), sem((2,)),
            message, message, message, message,
            flat(F32), flat(F32),
            pltpu.VMEM((PEERS, ROWS), BF16),
            pltpu.VMEM((2 * PEERS, ROWS), BF16),
            pltpu.VMEM((HALF + 16, ROWS), BF16),
            pltpu.VMEM((3, HALF // 2, STEP), BF16),
            pltpu.VMEM((4 * WINDOW, ROWS), BF16),
            pltpu.VMEM((6, LINES, 128), F32),
            pltpu.VMEM((16, ROWS), F32),
            pltpu.VMEM((LINES * NF, 128), F32),
            pltpu.VMEM((LINES * 8, 128), F32),
        ],
        compiler_params=pltpu.CompilerParams(
            collective_id=1, has_side_effects=True, vmem_limit_bytes=VMEM_LIMIT
        ),
        name="step",
    )(
        lines(owner), forcing, lines(sunlit), lines(plant_type), lines(leaf_area), soil_water, pft_table,
        lines(area), lines(column),
    )


def solution(mesh):
    spec = P(("row", "col"))
    wide = P(None, ("row", "col"))
    return jax.shard_map(
        body,
        mesh=mesh,
        in_specs=(wide, spec, spec, spec, spec, spec, spec, wide, P()),
        out_specs=(wide, wide),
        check_vma=False,
    )
```

time: 47.6 us -> 36.5 us (0.77)
  Pallas kernels: 43.5 us -> 32.4 us
    pallas_call x1, Pallas kernels: 43.5 us -> 32.4 us  [body(): pl.pallas_call(step_kernel, out_shape=(jax.ShapeDtypeStruct((NOUT, ROWS /...]
where the time goes in v3:
time: 36.5 us; the launch traced here: 36.3 us
  Pallas kernels  32.4 us (89%)
  local copies, waits for them, and re-layouts  3.24 us (9%)
  between operations  0.64 us (2%)
    pallas_call x1, Pallas kernels, body(): pl.pallas_call(step_kernel, out_shape=(jax.ShapeDtypeStruct((NOUT, ROWS /...  32.4 us
    unnamed x2, local copies, waits for them, and re-layouts  3.24 us

profile of v3, /device:TPU:1, one launch (start us, length us, event | category | flops | bytes accessed | tf_op | source)
XLA Modules:
  0.0 36.3 jit_solution(13979494773386563729)
XLA Ops:
  0.6 32.4 %step.1 = (f32[4,2048]{1,0:T(4,128)}, f32[15,8192]{1,0:T(8,128)}) custom-call(s32[64,128]{1,0:T(8,128)} %bitcast.6, bf16[8,8192]{1,0:T(8,128)(2,1)} %forcing_hbm.1, s32[64,128]{1,0:T(8,128)} %bitcast.7, s32[64,128]{1,0:T(8,128)} %bitcast.8, f32[64,128]{1,0:T(8,128)} %bitcast.9, f32[15,8192]{1,0:T(8,128)} %soil_hbm.1, f32[4,16]{1,0:T(4,128)} %table_hbm.1, ...), custom_call_target="tpu_custom_call" | custom-call | tf_op jit(solution)/shard_map/step/pallas_call | solution.py:415
  33.0 1.4 %copy.13 = f32[4,2048]{1,0:T(4,128)} copy(f32[4,2048]{1,0:T(4,128)} %get-tuple-element.4) | data formatting | bytes 65536
  34.4 1.9 %copy.14 = f32[15,8192]{1,0:T(8,128)} copy(f32[15,8192]{1,0:T(8,128)} %get-tuple-element.5) | data formatting | bytes 983040

commit v4 on v3

--- a/solution.py
+++ b/solution.py
@@ -24,6 +24,7 @@
 WINDOW = 64
 SENT = NF * SLOTS // 128
 BACK = 3
+PARTS = 4
 MESH = pl.DeviceIdType.MESH
 F32 = jnp.float32
 BF16 = jnp.bfloat16
@@ -314,21 +315,26 @@
             jnp.where((2 * k + line // NOUT).astype(F32) == quad, flux, 0.0) for k in range(QUADS // 2)
         ]
         w_ref[: NOUT * QUADS, 128 * j : 128 * (j + 1)] = jnp.concatenate(parts, axis=0).astype(BF16)
-    low = iota((NOUT * QUADS, 128), 1)
-    total = [[], [], [], []]
+    held = []
     for w in range(3):
         mine = [c for c in range(CHUNKS) if window_of(c) == w]
         lanes = slice(mine[0] * STEP, (mine[-1] + 1) * STEP)
-        g = dot_nt(w_ref[: NOUT * QUADS, lanes], p_ref[:, lanes])
-        for k in range(4):
-            half = g[:, 128 * (k // 2) : 128 * (k // 2 + 1)]
-            start = WINDOW * (k % 2)
-            half = jnp.where((low >= start) & (low < start + WINDOW), half, 0.0)
-            shift = (32 * w - start) % 128
-            total[k].append(pltpu.roll(half, shift, 1) if shift else half)
-    values = [a + b + c for a, b, c in total]
-    values.append(jnp.zeros((BACK * 128 - NOUT * SLOTS, PEERS), F32))
-    fold(jnp.concatenate(values, axis=0), msg_ref, BACK)
+        held.append(dot_nt(p_ref[:, lanes], w_ref[: NOUT * QUADS, lanes]))
+    parts = []
+    for k in range(4):
+        a, b, c = (g[WINDOW * k : WINDOW * (k + 1)] for g in held)
+        rows = jnp.concatenate([a[:32], a[32:] + b[:32], b[32:] + c[:32], c[32:]], axis=0)
+        rows = jnp.concatenate([rows, jnp.zeros((PEERS, 128 - NOUT * QUADS), F32)], axis=1)
+        shift = NOUT * QUADS * k % 128
+        parts.append(pltpu.roll(rows, shift, 1) if shift else rows)
+    lane = iota((PEERS, 128), 1)
+    lines = (
+        jnp.where(lane < 80, parts[0], parts[1]),
+        jnp.where(lane < 32, parts[1], jnp.where(lane < 112, parts[2], parts[3])),
+        parts[3],
+    )
+    for i in range(BACK):
+        msg_ref[pl.ds(i, PEERS, stride=8), :] = lines[i]
 
 
 def targets(column_ref, target_ref):
@@ -337,7 +343,7 @@
         target_ref[:, 128 * j : 128 * (j + 1)] = as_bf16(ids == column_ref[j : j + 1, :])
 
 
-def gather(home_ref, pair_ref, area_ref, split_ref, target_ref, atm_ref):
+def gather(home_ref, pair_ref, area_ref, split_ref, target_ref, atm_ref, both_ref):
     got = unfold(home_ref, BACK)
     rows = NOUT * QUADS
     part = lambda k: got[rows * k : rows * (k + 1), :]
@@ -345,19 +351,19 @@
     odd = jnp.concatenate([part(1), part(3)], axis=0)
     lhs = jnp.concatenate([even, odd], axis=1).astype(BF16)
     line = iota((8, STEP), 0)
+    for c in range(CHUNKS):
+        g = dot(lhs, split_ref[:, c * STEP : (c + 1) * STEP])
+        pair = jnp.broadcast_to(two_lines(pair_ref, c), (8, STEP))
+        value = jnp.zeros((8, STEP), F32)
+        for k in range(QUADS):
+            label = 2 * (2 * (k % (QUADS // 2)) + line // NOUT) + k // (QUADS // 2)
+            value = value + jnp.where(label.astype(F32) == pair, g[8 * k : 8 * (k + 1), :], 0.0)
+        value = (value + pltpu.roll(value, NOUT, 0)) * two_lines(area_ref, c)
+        high = value.astype(BF16).astype(F32)
+        both_ref[:, c * STEP : (c + 1) * STEP] = jnp.where(line < NOUT, high, value - high)
     for b in range(ROWS // BROWS):
-        both = []
-        for c in (2 * b, 2 * b + 1):
-            g = dot(lhs, split_ref[:, c * STEP : (c + 1) * STEP])
-            pair = jnp.broadcast_to(two_lines(pair_ref, c), (8, STEP))
-            value = jnp.zeros((8, STEP), F32)
-            for k in range(QUADS):
-                label = 2 * (2 * (k % (QUADS // 2)) + line // NOUT) + k // (QUADS // 2)
-                value = value + jnp.where(label.astype(F32) == pair, g[8 * k : 8 * (k + 1), :], 0.0)
-            value = (value + pltpu.roll(value, NOUT, 0)) * two_lines(area_ref, c)
-            high = value.astype(BF16).astype(F32)
-            both.append(jnp.where(line < NOUT, high, value - high).astype(BF16))
-        total = dot_nt(jnp.concatenate(both, axis=1), target_ref[:, b * BROWS : (b + 1) * BROWS])
+        lanes = slice(b * BROWS, (b + 1) * BROWS)
+        total = dot_nt(both_ref[:, lanes].astype(BF16), target_ref[:, lanes])
         atm_ref[:, BCOLS * b : BCOLS * (b + 1)] = total[:NOUT] + total[NOUT:]
 
 
@@ -368,6 +374,7 @@
     in_sem, out_sem, send_sem, recv_sem,
     msg_ref, got_ref, reply_ref, home_ref,
     pair_ref, quad_ref, a_ref, split_ref, w_ref, lhs_ref, p_ref, early_ref, draw_ref, field_ref, flux_ref,
+    both_ref,
 ):
     copies = [
         pltpu.make_async_copy(a, b, in_sem.at[i])
@@ -402,8 +409,24 @@
     after.start()
     targets(column_ref, a_ref)
     await_all(reply_ref, home_ref, BACK, send_sem.at[1], recv_sem.at[1])
-    gather(home_ref, pair_ref, area_ref, split_ref, a_ref, atm_ref)
+    gather(home_ref, pair_ref, area_ref, split_ref, a_ref, atm_ref, both_ref)
     after.wait()
+
+
+def hand_on_kernel(atm_ref, after_ref, atm_out, after_out, atm_buf, after_buf, in_sem, out_sem):
+    pairs = [(atm_ref, atm_buf, atm_out)]
+    for i in range(PARTS):
+        lanes = pl.ds(i * (ROWS // PARTS), ROWS // PARTS)
+        pairs.append(tuple(ref.at[:, lanes] for ref in (after_ref, after_buf, after_out)))
+    inward = [pltpu.make_async_copy(a, b, in_sem.at[i]) for i, (a, b, _) in enumerate(pairs)]
+    outward = [pltpu.make_async_copy(b, c, out_sem.at[i]) for i, (_, b, c) in enumerate(pairs)]
+    for copy in inward:
+        copy.start()
+    for one, two in zip(inward, outward):
+        one.wait()
+        two.start()
+    for copy in outward:
+        copy.wait()
 
 
 def body(forcing, owner, column, area, sunlit, plant_type, leaf_area, soil_water, pft_table):
@@ -412,7 +435,7 @@
     flat = lambda dtype: pltpu.VMEM((LINES, 128), dtype)
     message = pltpu.VMEM((PEERS * 8, 128), F32)
     sem = pltpu.SemaphoreType.DMA
-    return pl.pallas_call(
+    atm_flux, soil_after = pl.pallas_call(
         step_kernel,
         out_shape=(
             jax.ShapeDtypeStruct((NOUT, ROWS // BROWS * BCOLS), F32),
@@ -435,6 +458,7 @@
             pltpu.VMEM((16, ROWS), F32),
             pltpu.VMEM((LINES * NF, 128), F32),
             pltpu.VMEM((LINES * 8, 128), F32),
+            pltpu.VMEM((8, ROWS), F32),
         ],
         compiler_params=pltpu.CompilerParams(
             collective_id=1, has_side_effects=True, vmem_limit_bytes=VMEM_LIMIT
@@ -444,6 +468,20 @@
         lines(owner), forcing, lines(sunlit), lines(plant_type), lines(leaf_area), soil_water, pft_table,
         lines(area), lines(column),
     )
+    return pl.pallas_call(
+        hand_on_kernel,
+        out_shape=(
+            jax.ShapeDtypeStruct(atm_flux.shape, F32),
+            jax.ShapeDtypeStruct(soil_after.shape, F32),
+        ),
+        in_specs=[pl.BlockSpec(memory_space=pl.ANY)] * 2,
+        out_specs=(pl.BlockSpec(memory_space=pl.ANY),) * 2,
+        scratch_shapes=[
+            pltpu.VMEM(atm_flux.shape, F32), pltpu.VMEM(soil_after.shape, F32), sem((PARTS + 1,)), sem((PARTS + 1,)),
+        ],
+        compiler_params=pltpu.CompilerParams(vmem_limit_bytes=VMEM_LIMIT),
+        name="hand_on",
+    )(atm_flux, soil_after)
 
 
 def solution(mesh):

time: 36.5 us -> 33.8 us (0.926)
  local copies, waits for them, and re-layouts: 3.24 us -> 0 us
  Pallas kernels: 32.4 us -> 33 us
    unnamed x2 -> x0, local copies, waits for them, and re-layouts: 3.24 us -> none
    pallas_call x0 -> x1, Pallas kernels: none -> 1.86 us  [body(): pl.pallas_call(hand_on_kernel, out_shape=(jax.ShapeDtypeStruct(atm_flux.s...]
    pallas_call x1, Pallas kernels: 32.4 us -> 31.2 us  [body(): pl.pallas_call(step_kernel, out_shape=(jax.ShapeDtypeStruct((NOUT, ROWS /...]
where the time goes in v4:
time: 33.8 us; the launch traced here: 33.7 us
  Pallas kernels  33 us (98%)
  between operations  0.64 us (2%)
    pallas_call x1, Pallas kernels, body(): pl.pallas_call(step_kernel, out_shape=(jax.ShapeDtypeStruct((NOUT, ROWS /...  31.2 us
    pallas_call x1, Pallas kernels, body(): pl.pallas_call(hand_on_kernel, out_shape=(jax.ShapeDtypeStruct(atm_flux.s...  1.86 us

profile of v4, /device:TPU:1, one launch (start us, length us, event | category | flops | bytes accessed | tf_op | source)
XLA Modules:
  0.0 33.7 jit_solution(10539149272508269150)
XLA Ops:
  0.6 31.2 %step.1 = (f32[4,2048]{1,0:T(4,128)}, f32[15,8192]{1,0:T(8,128)}) custom-call(s32[64,128]{1,0:T(8,128)} %bitcast.6, bf16[8,8192]{1,0:T(8,128)(2,1)} %forcing_hbm.1, s32[64,128]{1,0:T(8,128)} %bitcast.7, s32[64,128]{1,0:T(8,128)} %bitcast.8, f32[64,128]{1,0:T(8,128)} %bitcast.9, f32[15,8192]{1,0:T(8,128)} %soil_hbm.1, f32[4,16]{1,0:T(4,128)} %table_hbm.1, ...), custom_call_target="tpu_custom_call" | custom-call | tf_op jit(solution)/shard_map/step/pallas_call | solution.py:438
  31.8 1.9 %hand_on.1 = (f32[4,2048]{1,0:T(4,128)}, f32[15,8192]{1,0:T(8,128)}) custom-call(f32[4,2048]{1,0:T(4,128)} %get-tuple-element.4.atm_ref, f32[15,8192]{1,0:T(8,128)} %get-tuple-element.5.after_ref), custom_call_target="tpu_custom_call" | custom-call | tf_op jit(solution)/shard_map/hand_on/pallas_call | solution.py:471

commit v5 on v4

--- a/solution.py
+++ b/solution.py
@@ -84,7 +84,9 @@
         pl.semaphore_signal(barrier, inc=1, device_id=neighbour(here, offset), device_id_type=MESH)
 
 
-def block(ref, index, lines):
+def slot_of(ref, index, lines):
+    if ref.dtype == BF16:
+        return ref.at[index]
     return ref.at[pl.ds(pl.multiple_of(index * 8, 8), lines), :]
 
 
@@ -94,33 +96,34 @@
     for offset in OFFSETS:
         row, col = neighbour(here, offset)
         pltpu.make_async_remote_copy(
-            src_ref=block(msg_ref, row * 16 + col, lines),
-            dst_ref=block(got_ref, me, lines),
+            src_ref=slot_of(msg_ref, row * 16 + col, lines),
+            dst_ref=slot_of(got_ref, me, lines),
             send_sem=send_sem,
             recv_sem=recv_sem,
             device_id=(row, col),
             device_id_type=MESH,
         ).start()
-    pltpu.make_async_copy(block(msg_ref, me, lines), block(got_ref, me, lines), recv_sem).start()
+    pltpu.make_async_copy(slot_of(msg_ref, me, lines), slot_of(got_ref, me, lines), recv_sem).start()
 
 
 def await_all(msg_ref, got_ref, lines, send_sem, recv_sem):
-    sent = msg_ref.at[: (PEERS - 1) * lines, :]
+    unit = 1 if msg_ref.dtype == BF16 else lines
+    sent = msg_ref.at[: (PEERS - 1) * unit]
     pltpu.make_async_copy(sent, sent, send_sem).wait()
-    got = got_ref.at[: PEERS * lines, :]
+    got = got_ref.at[: PEERS * unit]
     pltpu.make_async_copy(got, got, recv_sem).wait()
 
 
-def fold(values, msg_ref, lines):
-    for i in range(lines):
-        msg_ref[pl.ds(i, PEERS, stride=8), :] = values[128 * i : 128 * (i + 1), :].T
-
-
-def unfold(got_ref, lines):
-    return jnp.concatenate([got_ref[pl.ds(i, PEERS, stride=8), :].T for i in range(lines)], axis=0)
-
-
-def pack(owner_ref, forcing_ref, msg_ref, pair_ref, a_ref, split_ref, w_ref):
+def fold(lines, flat_ref):
+    for i, line in enumerate(lines):
+        flat_ref[pl.ds(i, PEERS, stride=8), :] = line
+
+
+def unfold(flat_ref, lines):
+    return jnp.concatenate([flat_ref[pl.ds(i, PEERS, stride=8), :].T for i in range(lines)], axis=0)
+
+
+def pack(owner_ref, forcing_ref, flat_ref, msg_ref, pair_ref, a_ref, split_ref, w_ref):
     ids = iota((PEERS, 128), 0)
     for j in range(LINES):
         a_ref[:, 128 * j : 128 * (j + 1)] = as_bf16(ids == owner_ref[j : j + 1, :])
@@ -160,7 +163,10 @@
         jnp.where((label + odd).astype(F32) < counts, got[:HALF, PEERS * odd : PEERS * (odd + 1)], -1.0)
         for odd in range(2)
     ]
-    fold(jnp.concatenate(values, axis=0), msg_ref, SENT)
+    values = jnp.concatenate(values, axis=0)
+    lines = [values[128 * i : 128 * (i + 1), :].T for i in range(SENT)]
+    fold(lines + [jnp.zeros((PEERS, 128), F32)], flat_ref)
+    msg_ref[...] = flat_ref[...].reshape(PEERS, 8, 128)[:, : SENT + 1].astype(BF16)
 
 
 def look(row, kinds):
@@ -199,8 +205,10 @@
     raise ValueError
 
 
-def arrange(got_ref, lhs_ref):
-    got = unfold(got_ref, SENT)
+def arrange(got_ref, flat_ref, lhs_ref):
+    got = jnp.concatenate([got_ref[...].astype(F32), jnp.zeros((PEERS, 2, 128), F32)], axis=1)
+    flat_ref[...] = got.reshape(PEERS * 8, 128)
+    got = unfold(flat_ref, SENT)
     valid = jnp.where(got >= 0.0, 1.0 / NF, 0.0)
     counts = jnp.sum(valid, axis=0, keepdims=True)
     part = lambda odd, a: got[HALF * odd + HALF // 2 * a : HALF * odd + HALF // 2 * (a + 1), :]
@@ -219,8 +227,8 @@
     return begin, end
 
 
-def unpack(got_ref, lhs_ref, p_ref, quad_ref, field_ref):
-    begin, end = arrange(got_ref, lhs_ref)
+def unpack(got_ref, flat_ref, lhs_ref, p_ref, quad_ref, field_ref):
+    begin, end = arrange(got_ref, flat_ref, lhs_ref)
     for c in range(CHUNKS):
         w = window_of(c)
         first = begin[32 * w : 32 * w + WINDOW]
@@ -333,8 +341,7 @@
         jnp.where(lane < 32, parts[1], jnp.where(lane < 112, parts[2], parts[3])),
         parts[3],
     )
-    for i in range(BACK):
-        msg_ref[pl.ds(i, PEERS, stride=8), :] = lines[i]
+    fold(lines, msg_ref)
 
 
 def targets(column_ref, target_ref):
@@ -372,7 +379,7 @@
     atm_ref, after_hbm,
     owner_ref, forcing_ref, sunlit_ref, type_ref, leaf_ref, soil_ref, table_ref, area_ref, column_ref,
     in_sem, out_sem, send_sem, recv_sem,
-    msg_ref, got_ref, reply_ref, home_ref,
+    msg_ref, got_ref, reply_ref, home_ref, flat_ref,
     pair_ref, quad_ref, a_ref, split_ref, w_ref, lhs_ref, p_ref, early_ref, draw_ref, field_ref, flux_ref,
     both_ref,
 ):
@@ -392,14 +399,14 @@
     greet(here)
     copies[0].wait()
     copies[1].wait()
-    pack(owner_ref, forcing_ref, msg_ref, pair_ref, a_ref, split_ref, w_ref)
+    pack(owner_ref, forcing_ref, flat_ref, msg_ref, pair_ref, a_ref, split_ref, w_ref)
     pl.semaphore_wait(pltpu.get_barrier_semaphore(), PEERS - 1)
     send_all(here, msg_ref, got_ref, SENT, send_sem.at[0], recv_sem.at[0])
     for copy in copies[2:]:
         copy.wait()
     prepare(sunlit_ref, type_ref, leaf_ref, table_ref, early_ref, draw_ref)
     await_all(msg_ref, got_ref, SENT, send_sem.at[0], recv_sem.at[0])
-    unpack(got_ref, lhs_ref, p_ref, quad_ref, field_ref)
+    unpack(got_ref, flat_ref, lhs_ref, p_ref, quad_ref, field_ref)
     physics(early_ref, field_ref, flux_ref)
     drain(soil_ref, draw_ref, flux_ref)
     reply(flux_ref, quad_ref, p_ref, w_ref, reply_ref)
@@ -433,7 +440,8 @@
     lines = lambda x: x.reshape(LINES, 128)
     i32 = jnp.int32
     flat = lambda dtype: pltpu.VMEM((LINES, 128), dtype)
-    message = pltpu.VMEM((PEERS * 8, 128), F32)
+    there = pltpu.VMEM((PEERS, SENT + 1, 128), BF16)
+    back = pltpu.VMEM((PEERS * 8, 128), F32)
     sem = pltpu.SemaphoreType.DMA
     atm_flux, soil_after = pl.pallas_call(
         step_kernel,
@@ -447,7 +455,7 @@
             flat(i32), pltpu.VMEM((NF, ROWS), BF16), flat(i32), flat(i32), flat(F32),
             pltpu.VMEM((LEVELS, ROWS), F32), pltpu.VMEM((4, NPFT), F32), flat(F32), flat(i32),
             sem((9,)), sem, sem((2,)), sem((2,)),
-            message, message, message, message,
+            there, there, back, back, back,
             flat(F32), flat(F32),
             pltpu.VMEM((PEERS, ROWS), BF16),
             pltpu.VMEM((2 * PEERS, ROWS), BF16),

time: 33.8 us -> 33.3 us (0.985)
  Pallas kernels: 33 us -> 32.5 us
    pallas_call x1, Pallas kernels: 31.2 us -> 30.6 us  [body(): pl.pallas_call(step_kernel, out_shape=(jax.ShapeDtypeStruct((NOUT, ROWS /...]
where the time goes in v5:
time: 33.3 us; the launch traced here: 33.1 us
  Pallas kernels  32.5 us (98%)
  between operations  0.64 us (2%)
    pallas_call x1, Pallas kernels, body(): pl.pallas_call(step_kernel, out_shape=(jax.ShapeDtypeStruct((NOUT, ROWS /...  30.6 us
    pallas_call x1, Pallas kernels, body(): pl.pallas_call(hand_on_kernel, out_shape=(jax.ShapeDtypeStruct(atm_flux.s...  1.86 us

profile of v5, /device:TPU:1, one launch (start us, length us, event | category | flops | bytes accessed | tf_op | source)
XLA Modules:
  0.0 33.1 jit_solution(17948389935803738685)
XLA Ops:
  0.6 30.6 %step.1 = (f32[4,2048]{1,0:T(4,128)}, f32[15,8192]{1,0:T(8,128)}) custom-call(s32[64,128]{1,0:T(8,128)} %bitcast.6, bf16[8,8192]{1,0:T(8,128)(2,1)} %forcing_hbm.1, s32[64,128]{1,0:T(8,128)} %bitcast.7, s32[64,128]{1,0:T(8,128)} %bitcast.8, f32[64,128]{1,0:T(8,128)} %bitcast.9, f32[15,8192]{1,0:T(8,128)} %soil_hbm.1, f32[4,16]{1,0:T(4,128)} %table_hbm.1, ...), custom_call_target="tpu_custom_call" | custom-call | tf_op jit(solution)/shard_map/step/pallas_call | solution.py:446
  31.3 1.9 %hand_on.1 = (f32[4,2048]{1,0:T(4,128)}, f32[15,8192]{1,0:T(8,128)}) custom-call(f32[4,2048]{1,0:T(4,128)} %get-tuple-element.4.atm_ref, f32[15,8192]{1,0:T(8,128)} %get-tuple-element.5.after_ref), custom_call_target="tpu_custom_call" | custom-call | tf_op jit(solution)/shard_map/hand_on/pallas_call | solution.py:479

commit v6 on v5

--- a/solution.py
+++ b/solution.py
@@ -166,7 +166,7 @@
     values = jnp.concatenate(values, axis=0)
     lines = [values[128 * i : 128 * (i + 1), :].T for i in range(SENT)]
     fold(lines + [jnp.zeros((PEERS, 128), F32)], flat_ref)
-    msg_ref[...] = flat_ref[...].reshape(PEERS, 8, 128)[:, : SENT + 1].astype(BF16)
+    msg_ref[...] = flat_ref[: PEERS * 8, :].reshape(PEERS, 8, 128)[:, : SENT + 1].astype(BF16)
 
 
 def look(row, kinds):
@@ -207,7 +207,7 @@
 
 def arrange(got_ref, flat_ref, lhs_ref):
     got = jnp.concatenate([got_ref[...].astype(F32), jnp.zeros((PEERS, 2, 128), F32)], axis=1)
-    flat_ref[...] = got.reshape(PEERS * 8, 128)
+    flat_ref[: PEERS * 8, :] = got.reshape(PEERS * 8, 128)
     got = unfold(flat_ref, SENT)
     valid = jnp.where(got >= 0.0, 1.0 / NF, 0.0)
     counts = jnp.sum(valid, axis=0, keepdims=True)
@@ -441,7 +441,7 @@
     i32 = jnp.int32
     flat = lambda dtype: pltpu.VMEM((LINES, 128), dtype)
     there = pltpu.VMEM((PEERS, SENT + 1, 128), BF16)
-    back = pltpu.VMEM((PEERS * 8, 128), F32)
+    back = pltpu.VMEM((PEERS * 8 + 8, 128), F32)
     sem = pltpu.SemaphoreType.DMA
     atm_flux, soil_after = pl.pallas_call(
         step_kernel,
@@ -464,8 +464,8 @@
             pltpu.VMEM((4 * WINDOW, ROWS), BF16),
             pltpu.VMEM((6, LINES, 128), F32),
             pltpu.VMEM((16, ROWS), F32),
-            pltpu.VMEM((LINES * NF, 128), F32),
-            pltpu.VMEM((LINES * 8, 128), F32),
+            pltpu.VMEM((LINES * NF + 8, 128), F32),
+            pltpu.VMEM((LINES * 8 + 8, 128), F32),
             pltpu.VMEM((8, ROWS), F32),
         ],
         compiler_params=pltpu.CompilerParams(

time: 33.3 us -> 33.3 us (level)
  no operation moved by 1% of the time
where the time goes in v6:
time: 33.3 us; the launch traced here: 33.1 us
  Pallas kernels  32.5 us (98%)
  between operations  0.64 us (2%)
    pallas_call x1, Pallas kernels, body(): pl.pallas_call(step_kernel, out_shape=(jax.ShapeDtypeStruct((NOUT, ROWS /...  30.6 us
    pallas_call x1, Pallas kernels, body(): pl.pallas_call(hand_on_kernel, out_shape=(jax.ShapeDtypeStruct(atm_flux.s...  1.86 us

profile of v6, /device:TPU:1, one launch (start us, length us, event | category | flops | bytes accessed | tf_op | source)
XLA Modules:
  0.0 33.1 jit_solution(8534548259004739673)
XLA Ops:
  0.6 30.6 %step.1 = (f32[4,2048]{1,0:T(4,128)}, f32[15,8192]{1,0:T(8,128)}) custom-call(s32[64,128]{1,0:T(8,128)} %bitcast.6, bf16[8,8192]{1,0:T(8,128)(2,1)} %forcing_hbm.1, s32[64,128]{1,0:T(8,128)} %bitcast.7, s32[64,128]{1,0:T(8,128)} %bitcast.8, f32[64,128]{1,0:T(8,128)} %bitcast.9, f32[15,8192]{1,0:T(8,128)} %soil_hbm.1, f32[4,16]{1,0:T(4,128)} %table_hbm.1, ...), custom_call_target="tpu_custom_call" | custom-call | tf_op jit(solution)/shard_map/step/pallas_call | solution.py:446
  31.3 1.9 %hand_on.1 = (f32[4,2048]{1,0:T(4,128)}, f32[15,8192]{1,0:T(8,128)}) custom-call(f32[4,2048]{1,0:T(4,128)} %get-tuple-element.4.atm_ref, f32[15,8192]{1,0:T(8,128)} %get-tuple-element.5.after_ref), custom_call_target="tpu_custom_call" | custom-call | tf_op jit(solution)/shard_map/hand_on/pallas_call | solution.py:479

commit v7 on v6

--- a/solution.py
+++ b/solution.py
@@ -350,7 +350,7 @@
         target_ref[:, 128 * j : 128 * (j + 1)] = as_bf16(ids == column_ref[j : j + 1, :])
 
 
-def gather(home_ref, pair_ref, area_ref, split_ref, target_ref, atm_ref, both_ref):
+def gather(home_ref, pair_ref, area_ref, split_ref, target_ref, atm_ref, both_ref, halves):
     got = unfold(home_ref, BACK)
     rows = NOUT * QUADS
     part = lambda k: got[rows * k : rows * (k + 1), :]
@@ -371,17 +371,19 @@
     for b in range(ROWS // BROWS):
         lanes = slice(b * BROWS, (b + 1) * BROWS)
         total = dot_nt(both_ref[:, lanes].astype(BF16), target_ref[:, lanes])
-        atm_ref[:, BCOLS * b : BCOLS * (b + 1)] = total[:NOUT] + total[NOUT:]
+        atm_ref[b // 8, :, BCOLS * (b % 8) : BCOLS * (b % 8 + 1)] = total[:NOUT] + total[NOUT:]
+        if b % 8 == 7:
+            halves[b // 8].start()
 
 
 def step_kernel(
     owner_hbm, forcing_hbm, sunlit_hbm, type_hbm, leaf_hbm, soil_hbm, table_hbm, area_hbm, column_hbm,
-    atm_ref, after_hbm,
+    atm_hbm, after_hbm,
     owner_ref, forcing_ref, sunlit_ref, type_ref, leaf_ref, soil_ref, table_ref, area_ref, column_ref,
     in_sem, out_sem, send_sem, recv_sem,
     msg_ref, got_ref, reply_ref, home_ref, flat_ref,
     pair_ref, quad_ref, a_ref, split_ref, w_ref, lhs_ref, p_ref, early_ref, draw_ref, field_ref, flux_ref,
-    both_ref,
+    both_ref, atm_ref,
 ):
     copies = [
         pltpu.make_async_copy(a, b, in_sem.at[i])
@@ -412,11 +414,17 @@
     reply(flux_ref, quad_ref, p_ref, w_ref, reply_ref)
     send_all(here, reply_ref, home_ref, BACK, send_sem.at[1], recv_sem.at[1])
     soil(soil_ref, draw_ref, field_ref, flux_ref)
-    after = pltpu.make_async_copy(soil_ref, after_hbm, out_sem)
+    half = ROWS // BROWS * BCOLS // 2
+    halves = [
+        pltpu.make_async_copy(atm_ref.at[i], atm_hbm.at[:, pl.ds(i * half, half)], out_sem.at[i + 1]) for i in range(2)
+    ]
+    after = pltpu.make_async_copy(soil_ref, after_hbm, out_sem.at[0])
     after.start()
     targets(column_ref, a_ref)
     await_all(reply_ref, home_ref, BACK, send_sem.at[1], recv_sem.at[1])
-    gather(home_ref, pair_ref, area_ref, split_ref, a_ref, atm_ref, both_ref)
+    gather(home_ref, pair_ref, area_ref, split_ref, a_ref, atm_ref, both_ref, halves)
+    for copy in halves:
+        copy.wait()
     after.wait()
 
 
@@ -450,11 +458,11 @@
             jax.ShapeDtypeStruct((LEVELS, ROWS), F32),
         ),
         in_specs=[pl.BlockSpec(memory_space=pl.ANY)] * 9,
-        out_specs=(pl.BlockSpec(memory_space=pltpu.VMEM), pl.BlockSpec(memory_space=pl.ANY)),
+        out_specs=(pl.BlockSpec(memory_space=pl.ANY),) * 2,
         scratch_shapes=[
             flat(i32), pltpu.VMEM((NF, ROWS), BF16), flat(i32), flat(i32), flat(F32),
             pltpu.VMEM((LEVELS, ROWS), F32), pltpu.VMEM((4, NPFT), F32), flat(F32), flat(i32),
-            sem((9,)), sem, sem((2,)), sem((2,)),
+            sem((9,)), sem((3,)), sem((2,)), sem((2,)),
             there, there, back, back, back,
             flat(F32), flat(F32),
             pltpu.VMEM((PEERS, ROWS), BF16),
@@ -467,6 +475,7 @@
             pltpu.VMEM((LINES * NF + 8, 128), F32),
             pltpu.VMEM((LINES * 8 + 8, 128), F32),
             pltpu.VMEM((8, ROWS), F32),
+            pltpu.VMEM((2, NOUT, ROWS // BROWS * BCOLS // 2), F32),
         ],
         compiler_params=pltpu.CompilerParams(
             collective_id=1, has_side_effects=True, vmem_limit_bytes=VMEM_LIMIT

time: 33.3 us -> 33.3 us (level)
  no operation moved by 1% of the time
where the time goes in v7:
time: 33.3 us; the launch traced here: 33.1 us
  Pallas kernels  32.5 us (98%)
  between operations  0.64 us (2%)
    pallas_call x1, Pallas kernels, body(): pl.pallas_call(step_kernel, out_shape=(jax.ShapeDtypeStruct((NOUT, ROWS /...  30.6 us
    pallas_call x1, Pallas kernels, body(): pl.pallas_call(hand_on_kernel, out_shape=(jax.ShapeDtypeStruct(atm_flux.s...  1.86 us

profile of v7, /device:TPU:1, one launch (start us, length us, event | category | flops | bytes accessed | tf_op | source)
XLA Modules:
  0.0 33.1 jit_solution(2292364387183292971)
XLA Ops:
  0.6 30.6 %step.1 = (f32[4,2048]{1,0:T(4,128)}, f32[15,8192]{1,0:T(8,128)}) custom-call(s32[64,128]{1,0:T(8,128)} %bitcast.6, bf16[8,8192]{1,0:T(8,128)(2,1)} %forcing_hbm.1, s32[64,128]{1,0:T(8,128)} %bitcast.7, s32[64,128]{1,0:T(8,128)} %bitcast.8, f32[64,128]{1,0:T(8,128)} %bitcast.9, f32[15,8192]{1,0:T(8,128)} %soil_hbm.1, f32[4,16]{1,0:T(4,128)} %table_hbm.1, ...), custom_call_target="tpu_custom_call" | custom-call | tf_op jit(solution)/shard_map/step/pallas_call | solution.py:454
  31.3 1.9 %hand_on.1 = (f32[4,2048]{1,0:T(4,128)}, f32[15,8192]{1,0:T(8,128)}) custom-call(f32[4,2048]{1,0:T(4,128)} %get-tuple-element.4.atm_ref, f32[15,8192]{1,0:T(8,128)} %get-tuple-element.5.after_ref), custom_call_target="tpu_custom_call" | custom-call | tf_op jit(solution)/shard_map/hand_on/pallas_call | solution.py:488
